TPU v7x, 512 devices: a whole 4x8x8 slice. The times are simulated.
512 devices in a mesh: tm: 32 (over x, z), space: 16 (over y, core).
Axes of the slice: x: 4, y: 8, z: 8, core: 2. Of those that a mesh axis runs over, the one named last changes fastest.
Arguments:
- queries: bfloat16 [512, 32, 8, 2240], P('tm', 'space'), may hold values from -6 to 6
- keys: bfloat16 [512, 32, 8, 2240], P('tm', 'space'), may hold values from -12 to 12
- values: bfloat16 [512, 32, 8, 2240], P('tm', 'space'), may hold values from -6 to 6
- gain: float32 [2240], replicated, may hold values from 0.1 to 1.9
- conv_weight: float32 [9, 2240], replicated, may hold values from -2 to 2
Outputs:
- mixed: bfloat16 [512, 32, 8, 2240], P('tm', 'space')
All inputs are finite; a program needn't handle non-finite values.
Results may differ from a plain program's by a relative error of at most 0.005.
Values may be sent and summed in bfloat16 or wider, within the bound.
No kernel may reach another device: no remote copies, remote signals or barrier semaphores. Data moves between devices by JAX's collectives and lax.ppermute only.
A program may use at most 128 MiB of HBM per device.

v0:
```python
import jax
import jax.numpy as jnp
from jax import lax
from jax.sharding import PartitionSpec as P

HEAD_DIM = 112


EPS = 1e-06


def prefix(part, axis, combine, identity):
    place = lax.axis_index(axis)
    gathered = jax.tree.map(lambda a: lax.all_gather(a, axis), part)
    state = jax.tree.map(lambda a, e: jnp.zeros_like(a) + jnp.asarray(e, a.dtype), part, identity)

    def one(step, state):
        return combine(
            state, jax.tree.map(lambda a: lax.dynamic_index_in_dim(a, step, 0, False), gathered)
        )

    return lax.fori_loop(0, place, one, state)


def extended(shard, sides, width):
    for axis, dim in sides:
        size, length = (lax.axis_size(axis), shard.shape[dim])
        up = [(i, (i + 1) % size) for i in range(size - 1)]
        down = [(j, i) for i, j in up]
        last = lax.slice_in_dim(shard, length - width, length, axis=dim)
        first = lax.slice_in_dim(shard, 0, width, axis=dim)
        before = lax.ppermute(last, axis, up)
        after = lax.ppermute(first, axis, down)
        shard = jnp.concatenate([before, shard, after], axis=dim)
    return shard


def add_pair(earlier, later):
    return (earlier[0] + later[0], earlier[1] + later[1])


def shards(queries, keys, values, gain, conv_weight):
    frames, rows, cols, width = queries.shape
    head_count = width // HEAD_DIM
    kflat = jnp.maximum(keys, 0).reshape(-1, head_count, HEAD_DIM)
    vflat = values.reshape(-1, head_count, HEAD_DIM)
    local_state = jnp.einsum("thi,thj->hij", kflat, vflat, preferred_element_type=jnp.float32)
    local_ksum = jnp.sum(kflat, axis=0, dtype=jnp.float32)
    total_state, total_ksum = lax.psum((local_state, local_ksum), "space")
    zero_pair = (jnp.zeros_like(total_state), jnp.zeros_like(total_ksum))
    before_state, before_ksum = prefix((total_state, total_ksum), "tm", add_pair, zero_pair)
    prefix_state = before_state + total_state
    prefix_ksum = before_ksum + total_ksum
    qflat = jnp.maximum(queries, 0).astype(jnp.float32).reshape(-1, head_count, HEAD_DIM)
    numer = jnp.einsum("thi,hij->thj", qflat, prefix_state, precision=lax.Precision.HIGHEST)
    denom = jnp.einsum("thi,hi->th", qflat, prefix_ksum, precision=lax.Precision.HIGHEST) + EPS
    attn = (numer / denom[..., None]).reshape(frames, rows, cols, width)
    meansq = jnp.mean(attn * attn, axis=-1, keepdims=True)
    normed = (attn * lax.rsqrt(meansq + 1e-06) * gain).astype(jnp.bfloat16)
    padded = extended(normed, (("space", 1),), 1)
    padded = jnp.pad(padded, ((0, 0), (0, 0), (1, 1), (0, 0)))
    total = jnp.zeros((frames, rows, cols, width), jnp.float32)
    for row_off in range(3):
        for col_off in range(3):
            window = padded[:, row_off : row_off + rows, col_off : col_off + cols, :]
            total = total + window.astype(jnp.float32) * conv_weight[3 * row_off + col_off]
    return total.astype(jnp.bfloat16)


def solution(mesh):
    placed = (
        P("tm", "space", None, None),
        P("tm", "space", None, None),
        P("tm", "space", None, None),
        P(),
        P(),
    )
    return jax.shard_map(
        shards, mesh=mesh, in_specs=placed, out_specs=P("tm", "space", None, None), check_vma=False
    )
```

profile of v0, /device:TPU:479, one launch (start us, length us, event | category | flops | bytes accessed | tf_op | source)
XLA Modules:
  0.0 477.9 jit_solution(8115522810589944133)
XLA Ops:
  7.9 1.7 reshape.41
  9.6 3.1 reshape.42
  12.7 1.6 fusion.6
  14.3 117.3 %all-reduce.3.cloned.1.call-done = f32[20,112,112]{2,1,0:T(8,128)} async-done(((f32[20,112,112]{2,1,0:T(8,128)}), f32[20,112,112]{2,1,0:T(8,128)}) %all-reduce.3.cloned.1.call-update) | async-done | bytes 1003536 | tf_op jit(solution)/shard_map/psum | solution.py:49
  133.4 1.7 reshape.43
  136.1 47.3 %psum.15 = f32[20,112]{1,0:T(8,128)S(1)} all-reduce(f32[20,112]{1,0:T(8,128)S(1)} %reduce_sum.21), channel_id=1, replica_groups=mesh['tm'=32,'space'=16] {'space'}, use_global_device_ids=true, to_apply=%region_2.0 | all-reduce | flops 2240 | bytes 17920 | tf_op jit(solution)/shard_map/psum | solution.py:49
  183.4 38.1 %all-gather.2 = f32[32,20,112]{2,1,0:T(8,128)S(1)} all-gather(f32[1,20,112]{2,1,0:T(8,128)S(1)} %bitcast.29), channel_id=3, replica_groups=mesh['tm'=32,'space'=16] {'tm'}, dimensions={0}, use_global_device_ids=true | all-gather | bytes 295680 | tf_op jit(solution)/shard_map/all_gather | solution.py:14
  221.4 168.0 %all-gather.5.cloned.1.call-done = f32[640,112,112]{2,1,0:T(8,128)} async-done(((f32[20,112,112]{2,1,0:T(8,128)}), f32[640,112,112]{2,1,0:T(8,128)}) %all-gather.5.cloned.1.call-update) | async-done | bytes 32112656 | tf_op jit(solution)/shard_map/all_gather | solution.py:14
  389.5 48.0 %while.12 = (s32[]{:T(128)}, f32[20,112,112]{2,1,0:T(8,128)S(1)}, f32[20,112]{1,0:T(8,128)S(1)}, s32[]{:T(128)}, f32[32,20,112,112]{3,2,1,0:T(8,128)}, /*index=5...) while((s32[]{:T(128)}, f32[20,112,112]{2,1,0:T(8,128)S(1)}, f32[20,112]{1,0:T(8,128)S(1)}, ...), condition=%wide.region_4.5_spmd, body=%wide.region_3.4_spmd.sunk | while | flops 253125 | bytes 3037575 | solution.py:22
  389.5 1.5 bitcast_add_fusion.5
  391.1 1.5 bitcast_add_fusion.5
  392.6 1.5 bitcast_add_fusion.5
  394.2 1.5 bitcast_add_fusion.5
  395.7 1.5 bitcast_add_fusion.5
  397.3 1.5 bitcast_add_fusion.5
  398.8 1.5 bitcast_add_fusion.5
  400.4 1.5 bitcast_add_fusion.5
  401.9 1.5 bitcast_add_fusion.5
  403.4 1.5 bitcast_add_fusion.5
  405.0 1.5 bitcast_add_fusion.5
  406.5 1.5 bitcast_add_fusion.5
  408.1 1.5 bitcast_add_fusion.5
  409.6 1.5 bitcast_add_fusion.5
  411.2 1.5 bitcast_add_fusion.5
  412.7 1.5 bitcast_add_fusion.5
  414.3 1.5 bitcast_add_fusion.5
  415.8 1.5 bitcast_add_fusion.5
  417.4 1.5 bitcast_add_fusion.5
  418.9 1.5 bitcast_add_fusion.5
  420.5 1.5 bitcast_add_fusion.5
  422.0 1.5 bitcast_add_fusion.5
  423.6 1.5 bitcast_add_fusion.5
  425.1 1.5 bitcast_add_fusion.5
  426.6 1.5 bitcast_add_fusion.5
  428.2 1.5 bitcast_add_fusion.5
  429.7 1.5 bitcast_add_fusion.5
  431.3 1.5 bitcast_add_fusion.5
  432.8 1.5 bitcast_add_fusion.5
  438.0 3.9 multiply_reduce_fusion
  442.0 2.4 copy.20
  444.4 1.9 reshape.44
  446.4 2.0 multiply_convert_fusion
  448.5 4.7 collective-permute-start
  453.2 1.9 collective-permute-start.1
  455.3 4.6 collective-permute-done
  460.0 5.6 %collective-permute-done.1 = bf16[16,1,8,2240]{3,2,1,0:T(8,128)(2,1)S(1)} collective-permute-done((bf16[16,1,8,2240]{3,2,1,0:T(8,128)(2,1)S(1)}, bf16[16,1,8,2240]{3,2,1,0:T(8,128)(2,1)S(1)}, u32[]{:S(2)}, u32[]{:S(2)}) %collective-permute-start.1) | collective-permute-done | bytes 573472 | tf_op jit(solution)/shard_map/ppermute | solution.py:33
  465.6 2.0 fusion.5
  467.6 3.5 add_convert_fusion
  (57 shorter events, 8.5 us)
Async XLA Ops:
  6.5 125.1 %all-reduce.3.cloned.1.call-start = ((), (), s32[]{:S(2)}) async-start(), calls=%async_computation | async-start | bytes 2293760 | tf_op jit(solution)/shard_map/psum | solution.py:49
  14.3 117.4 %copy-start = (bf16[16,2,8,2240]{3,2,1,0:T(8,128)(2,1)S(1)}, bf16[16,2,8,2240]{3,2,1,0:T(8,128)(2,1)}, u32[]{:S(2)}) copy-start(bf16[16,2,8,2240]{3,2,1,0:T(8,128)(2,1)} %param.8) | copy-start | bytes 3440644
  14.3 375.1 %all-gather.5.cloned.1.call-start = ((), (), s32[]{:S(2)}) async-start(), calls=%async_computation.1 | async-start | bytes 37847040 | tf_op jit(solution)/shard_map/all_gather | solution.py:14
  444.3 2.1 copy-start.2
  446.4 8.7 %copy-start.1 = (f32[9,2240]{1,0:T(8,128)S(1)}, f32[9,2240]{1,0:T(8,128)}, u32[]{:S(2)}) copy-start(f32[9,2240]{1,0:T(8,128)} %param.11) | copy-start | bytes 241924
  448.5 11.5 %collective-permute-start = (bf16[16,1,8,2240]{3,2,1,0:T(8,128)(2,1)S(1)}, bf16[16,1,8,2240]{3,2,1,0:T(8,128)(2,1)S(1)}, u32[]{:S(2)}, u32[]{:S(2)}) collective-permute-start(bf16[16,1,8,2240]{3,2,1,0:T(8,128)(2,1)S(1)} %get-tuple-element.62), channel_id=1, source_target_pairs={{0,1},{1,2},{2,3},{3,4},{4,5},{5,6},{6,7},{7,8},{8,9},{9,10},{10,1... | collective-permute-start | bytes 1720328 | tf_op jit(solution)/shard_map/ppermute | solution.py:32
  453.2 12.4 %collective-permute-start.1 = (bf16[16,1,8,2240]{3,2,1,0:T(8,128)(2,1)S(1)}, bf16[16,1,8,2240]{3,2,1,0:T(8,128)(2,1)S(1)}, u32[]{:S(2)}, u32[]{:S(2)}) collective-permute-start(bf16[16,1,8,2240]{3,2,1,0:T(8,128)(2,1)S(1)} %get-tuple-element.63), channel_id=1, source_target_pairs={{1,0},{2,1},{3,2},{4,3},{5,4},{6,5},{7,6},{8,7},{9,8},{10,9},{11,1... | collective-permute-start | bytes 1720328 | tf_op jit(solution)/shard_map/ppermute | solution.py:33
Sparse Core Ops, SparseCore 0:
  14.4 117.1 all-reduce.2
  134.8 254.5 all-gather.4
where the time goes:
time: 479 us; the launch traced here: 478 us
  waiting for transfers between devices  296 us (62%)
  blocking collectives  85.4 us (18%)
  other arithmetic  57.3 us (12%)
  between operations  13.6 us (3%)
  local copies, waits for them, and re-layouts  12.3 us (3%)
  starting transfers between devices  6.66 us (1%)
  matrix products  6.06 us (1%)
    all_gather x1, waiting for transfers between devices, prefix(): gathered = jax.tree.map(lambda a: lax.all_gather(a, axis), part)  168 us
    psum x1, waiting for transfers between devices, shards(): total_state, total_ksum = lax.psum((local_state, local_ksum), 'space')  117 us
    psum x1, blocking collectives, shards(): total_state, total_ksum = lax.psum((local_state, local_ksum), 'space')  47.3 us
    add x62, other arithmetic, add_pair(): return (earlier[0] + later[0], earlier[1] + later[1])  46.9 us
    all_gather x1, blocking collectives, prefix(): gathered = jax.tree.map(lambda a: lax.all_gather(a, axis), part)  38.1 us
  transfers between devices with their start and end apart: 4, of which 4 were waited for; matrix products, arithmetic and copies ran while one was open for 1% of the time, Pallas kernels for 0%

commit v1 on v0

v1 whole, which is shorter than its diff:
```python
import jax
import jax.numpy as jnp
from jax import lax
from jax.experimental import pallas as pl
from jax.experimental.pallas import tpu as pltpu
from jax.sharding import Mesh, PartitionSpec as P

HEAD = 112
WIDTH = 2240
HEADS = WIDTH // HEAD
LANES = 128
TILES = 18
HALF_TILES = TILES // 2
HALF_ROWS = 1024
EPS = 1e-06
F32, BF16 = jnp.float32, jnp.bfloat16
VMEM_LIMIT = 48 * 1024 * 1024


def tile_heads(tile):
    first = tile + tile // 7
    return first, HEAD * (first + 1) - LANES * tile


def lane_range(tile):
    return LANES * tile, min(LANES * (tile + 1), WIDTH)


def state_kernel(core_ref, k_ref, v_ref, mine_ref, other_ref, kt_ref):
    core = core_ref[0]
    for tile in range(TILES):
        low, high = lane_range(tile)
        kt_ref[low:high, :] = jnp.maximum(k_ref[:, low:high], 0).T
    lane = lax.broadcasted_iota(jnp.int32, (HEAD, LANES), 1)
    ones = jnp.ones((k_ref.shape[0], LANES), BF16)
    for tile in range(TILES):
        first, end = tile_heads(tile)
        low, high = lane_range(tile)
        v = v_ref[:, low:high]
        if tile < TILES - 1:
            pair = jnp.dot(kt_ref[HEAD * first : HEAD * (first + 2), :], v, preferred_element_type=F32)
            state = jnp.where(lane < end, pair[:HEAD], pair[HEAD:])
        else:
            v = jnp.concatenate([v, jnp.zeros((v.shape[0], LANES - v.shape[1]), BF16)], axis=1)
            state = jnp.dot(kt_ref[HEAD * first : WIDTH, :], v, preferred_element_type=F32)
            for head in range(HEADS):
                ksum = jnp.dot(
                    kt_ref[HEAD * head : HEAD * (head + 1), :], ones, preferred_element_type=F32
                )
                state = jnp.where(lane == end + head, ksum, state)
        half, place = divmod(tile, HALF_TILES)
        rows = slice(HEAD * place, HEAD * (place + 1))

        @pl.when(core == half)
        def _():
            mine_ref[rows, :] = state

        @pl.when(core != half)
        def _():
            other_ref[rows, :] = state.astype(BF16)

    rest = slice(HEAD * HALF_TILES, HALF_ROWS)
    mine_ref[rest, :] = jnp.zeros((HALF_ROWS - HEAD * HALF_TILES, LANES), F32)
    other_ref[rest, :] = jnp.zeros((HALF_ROWS - HEAD * HALF_TILES, LANES), BF16)


def readout_kernel(core_ref, q_ref, mine_ref, other_ref, gain_ref, top_ref, low_ref, state_ref, attn_ref):
    core = core_ref[0]
    tokens = q_ref.shape[0]
    state_ref[core] = mine_ref[...]
    state_ref[1 - core] = other_ref[...]
    lane = lax.broadcasted_iota(jnp.int32, (HEAD, LANES), 1)
    zero = jnp.zeros((HEAD, LANES), BF16)

    def tile_state(tile):
        half, place = divmod(tile, HALF_TILES)
        return state_ref[half, HEAD * place : HEAD * (place + 1), :]

    last = tile_state(TILES - 1)
    last_end = tile_heads(TILES - 1)[1]
    square = jnp.zeros((tokens, LANES), F32)
    for tile in range(TILES):
        first, end = tile_heads(tile)
        heads = [h for h in (first, first + 1) if h < HEADS]
        state = tile_state(tile)
        start = HEAD * first // LANES * LANES
        stop = min(start + 3 * LANES, WIDTH)
        parts = []
        offset = HEAD * first - start
        if offset:
            parts.append(jnp.zeros((offset, 2 * LANES), BF16))
        for position, head in enumerate(heads):
            inside = (lane < end) if position == 0 else (lane >= end)
            ksum = jnp.broadcast_to(last[:, last_end + head : last_end + head + 1], (HEAD, LANES))
            parts.append(
                jnp.concatenate([jnp.where(inside, state, zero), jnp.where(inside, ksum, zero)], axis=1)
            )
        remain = stop - start - offset - HEAD * len(heads)
        if remain:
            parts.append(jnp.zeros((remain, 2 * LANES), BF16))
        weights = jnp.concatenate(parts, axis=0)
        q = jnp.maximum(q_ref[:, start:stop], 0)
        both = jnp.dot(q, weights, preferred_element_type=F32)
        attn = both[:, :LANES] / (both[:, LANES:] + EPS)
        if tile == TILES - 1:
            keep = lax.broadcasted_iota(jnp.int32, (tokens, LANES), 1) < end
            attn = jnp.where(keep, attn, 0.0)
        attn_ref[:, LANES * tile : LANES * (tile + 1)] = attn
        square = square + attn * attn
    scale = lax.rsqrt(jnp.sum(square, axis=1, keepdims=True) * (1.0 / WIDTH) + 1e-06)
    scale = jnp.broadcast_to(scale, (tokens, LANES))
    for tile in range(TILES):
        low, high = lane_range(tile)
        wide = high - low
        normed = attn_ref[:, low:high] * scale[:, :wide] * gain_ref[:, low:high]
        normed = normed.astype(BF16).astype(F32).reshape(tokens // 16, 2, 8, wide)
        top_ref[:, low:high] = normed[:, 0].reshape(tokens // 2, wide).astype(BF16)
        low_ref[:, low:high] = normed[:, 1].reshape(tokens // 2, wide).astype(BF16)


def conv_kernel(before_ref, top_ref, low_ref, after_ref, weight_ref, out_ref):
    tokens = top_ref.shape[0]
    frames = tokens // 8
    for tile in range(TILES):
        low, high = lane_range(tile)
        wide = high - low
        col = lax.broadcasted_iota(jnp.int32, (8, wide), 0)
        weights = []
        for tap in range(9):
            w = jnp.broadcast_to(weight_ref[tap : tap + 1, low:high], (8, wide))
            if tap % 3 == 0:
                w = jnp.where(col == 0, 0.0, w)
            if tap % 3 == 2:
                w = jnp.where(col == 7, 0.0, w)
            weights.append(w[None])
        totals = [jnp.zeros((frames, 8, wide), F32)] * 2
        for place, ref in enumerate((before_ref, top_ref, low_ref, after_ref)):
            row = ref[:, low:high].astype(F32).reshape(frames, 8, wide)
            moved = (pltpu.roll(row, 1, 1), row, pltpu.roll(row, 7, 1))
            for out_row in range(2):
                row_off = place - out_row
                if 0 <= row_off <= 2:
                    for col_off in range(3):
                        totals[out_row] = totals[out_row] + moved[col_off] * weights[3 * row_off + col_off]
        both = jnp.concatenate([totals[0][:, None], totals[1][:, None]], axis=1)
        out_ref[:, low:high] = both.reshape(2 * tokens, wide).astype(BF16)


def call(kernel, outs, in_specs, scratch=()):
    return pl.pallas_call(
        kernel,
        out_shape=outs,
        in_specs=in_specs,
        out_specs=jax.tree.map(lambda _: pl.BlockSpec(memory_space=pltpu.VMEM), outs),
        scratch_shapes=scratch,
        compiler_params=pltpu.CompilerParams(vmem_limit_bytes=VMEM_LIMIT),
    )


VM = pl.BlockSpec(memory_space=pltpu.VMEM)
SM = pl.BlockSpec(memory_space=pltpu.SMEM)


def shards(queries, keys, values, gain, conv_weight):
    frames, rows, cols, width = queries.shape
    tokens = frames * rows * cols
    shape = jax.ShapeDtypeStruct
    core = lax.axis_index("core").reshape(1).astype(jnp.int32)
    swap = [(0, 1), (1, 0)]

    mine, other = call(
        state_kernel,
        [shape((HALF_ROWS, LANES), F32), shape((HALF_ROWS, LANES), BF16)],
        [SM, VM, VM],
        [pltpu.VMEM((WIDTH, tokens), BF16)],
    )(core, keys.reshape(tokens, width), values.reshape(tokens, width))

    xs, ys, zs = lax.axis_size("x"), lax.axis_size("y"), lax.axis_size("z")
    chunk = HALF_ROWS // (xs * ys)
    half = (mine + lax.ppermute(other, "core", swap).astype(F32)).astype(BF16)
    pieces = lax.all_to_all(half.reshape(xs * ys, chunk, LANES), ("x", "y"), 0, 0, tiled=True)
    totals = jnp.sum(pieces.reshape(xs, ys, chunk, LANES).astype(F32), axis=1).astype(BF16)

    spread = jnp.broadcast_to(totals[None], (zs, xs, chunk, LANES))
    blocks = lax.all_to_all(spread, "z", 0, 0, tiled=True)
    earlier = (jnp.arange(zs) <= lax.axis_index("z")).astype(F32)[:, None, None, None]
    prefix = []
    before = jnp.zeros((chunk, LANES), F32)
    upto = jnp.sum(blocks.astype(F32) * earlier, axis=0)
    whole = jnp.sum(blocks.astype(F32), axis=0)
    for x in range(xs):
        prefix.append((before + upto[x]).astype(BF16))
        before = before + whole[x]
    prefix = jnp.broadcast_to(jnp.stack(prefix)[:, None], (xs, ys, chunk, LANES))
    held = lax.all_to_all(prefix.reshape(xs * ys, chunk, LANES), ("x", "y"), 0, 0, tiled=True)
    held = held.reshape(HALF_ROWS, LANES)
    taken = lax.ppermute(held, "core", swap)

    top, low = call(
        readout_kernel,
        [shape((tokens // 2, width), BF16)] * 2,
        [SM, VM, VM, VM, VM],
        [pltpu.VMEM((2, HALF_ROWS, LANES), BF16), pltpu.VMEM((tokens, TILES * LANES), F32)],
    )(core, queries.reshape(tokens, width), held, taken, gain.reshape(1, width))

    size = ys * 2
    up = [(i, i + 1) for i in range(size - 1)]
    down = [(i + 1, i) for i in range(size - 1)]
    before = lax.ppermute(low, ("y", "core"), up)
    after = lax.ppermute(top, ("y", "core"), down)
    out = call(conv_kernel, shape((tokens, width), BF16), [VM] * 5)(before, top, low, after, conv_weight)
    return out.reshape(frames, rows, cols, width)


def solution(mesh):
    fine = Mesh(mesh.devices.reshape(4, 8, 8, 2), ("x", "z", "y", "core"))
    tokens = P(("x", "z"), ("y", "core"), None, None)
    return jax.shard_map(
        shards, mesh=fine, in_specs=(tokens, tokens, tokens, P(), P()), out_specs=tokens, check_vma=False
    )
```

time: 479 us -> 94.4 us (0.20)
  the two profiles are of different devices: /device:TPU:479 before, /device:TPU:1 now
where the time goes in v1:
time: 94.4 us; the launch traced here: 93.9 us
  starting transfers between devices  30.8 us (33%)
  blocking collectives  30.7 us (33%)
  waiting for transfers between devices  18.3 us (19%)
  Pallas kernels  8.51 us (9%)
  local copies, waits for them, and re-layouts  5.21 us (6%)
    all_to_all x1, blocking collectives, shards(): lax.all_to_all(prefix.reshape(xs * ys, chunk, LANES), ('x', 'y'), 0, 0, t...  16.9 us
    all_to_all x1, blocking collectives, shards(): lax.all_to_all(half.reshape(xs * ys, chunk, LANES), ('x', 'y'), 0, 0, til...  13.8 us
    all_to_all x1, starting transfers between devices, shards(): blocks = lax.all_to_all(spread, 'z', 0, 0, tiled=True)  10 us
    all_to_all x1, waiting for transfers between devices, shards(): blocks = lax.all_to_all(spread, 'z', 0, 0, tiled=True)  9.37 us
    ppermute x1, starting transfers between devices, shards(): half = (mine + lax.ppermute(other, 'core', swap).astype(F32)).astype(BF16)  8.79 us
    ppermute x1, starting transfers between devices, shards(): taken = lax.ppermute(held, 'core', swap)  6.21 us
    ppermute x1, waiting for transfers between devices, shards(): after = lax.ppermute(top, ('y', 'core'), down)  4.28 us
    pallas_call x1, Pallas kernels, shards(): call(state_kernel, [shape((HALF_ROWS, LANES), F32), shape((HALF_ROWS, LAN...  3.94 us
  transfers between devices with their start and end apart: 5, of which 5 were waited for; matrix products, arithmetic and copies ran while one was open for 1% of the time, Pallas kernels for 0%

profile of v1, /device:TPU:1, one launch (start us, length us, event | category | flops | bytes accessed | tf_op | source)
XLA Modules:
  0.0 93.9 jit_solution(2311813728950346016)
XLA Ops:
  0.0 0.0 copy-start
  0.0 1.3 %copy-done = bf16[16,2,8,2240]{3,2,1,0:T(8,128)(2,1)S(1)} copy-done((bf16[16,2,8,2240]{3,2,1,0:T(8,128)(2,1)S(1)}, bf16[16,2,8,2240]{3,2,1,0:T(8,128)(2,1)}, u32[]{:S(2)}) %copy-start) | copy-done | bytes 1146904
  1.3 0.0 copy-start.1
  1.3 1.3 %copy-done.1 = bf16[16,2,8,2240]{3,2,1,0:T(8,128)(2,1)S(1)} copy-done((bf16[16,2,8,2240]{3,2,1,0:T(8,128)(2,1)S(1)}, bf16[16,2,8,2240]{3,2,1,0:T(8,128)(2,1)}, u32[]{:S(2)}) %copy-start.1) | copy-done | bytes 1146904
  2.5 3.9 %shard_map.55 = (f32[1024,128]{1,0:T(8,128)S(1)}, bf16[1024,128]{1,0:T(8,128)(2,1)S(1)}) custom-call(s32[1]{0:T(128)} %bitcast.core_ref, bf16[256,2240]{1,0:T(8,128)(2,1)S(1)} %bitcast.10, bf16[256,2240]{1,0:T(8,128)(2,1)S(1)} %bitcast.11), custom_call_target="tpu_custom_call" | custom-call | tf_op jit(solution)/shard_map/pallas_call | solution.py:171
  6.5 8.8 %collective-permute-start = (bf16[1024,128]{1,0:T(8,128)(2,1)S(1)}, bf16[1024,128]{1,0:T(8,128)(2,1)S(1)}, u32[]{:S(2)}, u32[]{:S(2)}) collective-permute-start(bf16[1024,128]{1,0:T(8,128)(2,1)S(1)} %get-tuple-element.10), channel_id=1, source_target_pairs={{0,1},{1,0},{2,3},{3,2},{4,5},{5,4},{6,7},{7,6},{8,9},{9,8},{10,11... | collective-permute-start | bytes 786440 | tf_op jit(solution)/shard_map/ppermute | solution.py:180
  15.3 1.1 %collective-permute-done = bf16[1024,128]{1,0:T(8,128)(2,1)S(1)} collective-permute-done((bf16[1024,128]{1,0:T(8,128)(2,1)S(1)}, bf16[1024,128]{1,0:T(8,128)(2,1)S(1)}, u32[]{:S(2)}, u32[]{:S(2)}) %collective-permute-start) | collective-permute-done | bytes 262176 | tf_op jit(solution)/shard_map/ppermute | solution.py:180
  16.4 0.1 add_convert_fusion
  16.5 13.8 %all_to_all.15 = bf16[32,32,128]{2,1,0:T(8,128)(2,1)S(1)} all-to-all(bf16[32,32,128]{2,1,0:T(8,128)(2,1)S(1)} %bitcast.16), channel_id=1, replica_groups=mesh['x'=4,'z'=8,'y'=8,'core'=2] {'x','y'}, dimensions={0} | all-to-all | bytes 524288 | tf_op jit(solution)/shard_map/all_to_all | solution.py:181
  30.3 0.0 copy-start.4
  30.3 0.0 copy-start.2
  30.3 0.7 broadcast_in_dim.4
  31.1 10.0 %all-to-all-start.1 = ((bf16[8,4,32,128]{3,2,1,0:T(8,128)(2,1)}), bf16[8,4,32,128]{3,2,1,0:T(8,128)(2,1)S(1)}, u32[]{:S(2)}, u32[]{:S(2)}) async-start(bf16[8,4,32,128]{3,2,1,0:T(8,128)(2,1)} %broadcast_in_dim.4), calls=%async_computation.1 | async-start | bytes 524288 | tf_op jit(solution)/shard_map/all_to_all | solution.py:185
  41.1 9.4 %all-to-all-done.1 = bf16[8,4,32,128]{3,2,1,0:T(8,128)(2,1)S(1)} async-done(((bf16[8,4,32,128]{3,2,1,0:T(8,128)(2,1)}), bf16[8,4,32,128]{3,2,1,0:T(8,128)(2,1)S(1)}, u32[]{:S(2)}, u32[]{:S(2)}) %all-to-all-start.1) | async-done | bytes 262176 | tf_op jit(solution)/shard_map/all_to_all | solution.py:185
  50.5 0.1 convert_reduce_fusion
  50.7 16.9 %all_to_all.16 = bf16[32,32,128]{2,1,0:T(8,128)(2,1)S(1)} all-to-all(bf16[32,32,128]{2,1,0:T(8,128)(2,1)S(1)} %bitcast.15), channel_id=1, replica_groups=mesh['x'=4,'z'=8,'y'=8,'core'=2] {'x','y'}, dimensions={0} | all-to-all | bytes 524288 | tf_op jit(solution)/shard_map/all_to_all | solution.py:195
  67.6 6.2 %collective-permute-start.1 = (bf16[1024,128]{1,0:T(8,128)(2,1)S(1)}, bf16[1024,128]{1,0:T(8,128)(2,1)S(1)}, u32[]{:S(2)}, u32[]{:S(2)}) collective-permute-start(bf16[1024,128]{1,0:T(8,128)(2,1)S(1)} %bitcast.13), channel_id=1, source_target_pairs={{0,1},{1,0},{2,3},{3,2},{4,5},{5,4},{6,7},{7,6},{8,9},{9,8},{10,11... | collective-permute-start | bytes 786440 | tf_op jit(solution)/shard_map/ppermute | solution.py:197
  73.9 0.0 copy-done.4
  73.9 1.1 %collective-permute-done.1.other_ref = bf16[1024,128]{1,0:T(8,128)(2,1)S(1)} collective-permute-done((bf16[1024,128]{1,0:T(8,128)(2,1)S(1)}, bf16[1024,128]{1,0:T(8,128)(2,1)S(1)}, u32[]{:S(2)}, u32[]{:S(2)}) %collective-permute-start.1) | collective-permute-done | bytes 262176 | tf_op jit(solution)/shard_map/ppermute | solution.py:197
  75.0 0.0 copy-done.2
  75.0 1.7 %shard_map.56 = (bf16[128,2240]{1,0:T(8,128)(2,1)S(1)}, bf16[128,2240]{1,0:T(8,128)(2,1)S(1)}) custom-call(s32[1]{0:T(128)} %bitcast.core_ref, bf16[256,2240]{1,0:T(8,128)(2,1)S(1)} %bitcast.12, bf16[1024,128]{1,0:T(8,128)(2,1)S(1)} %bitcast.14, bf16[1024,128]{1,0:T(8,128)(2,1)S(1)} %collective-permute-done.1.other_ref, f32[1,2240]{1,0:T(1,128)S(1)} %reshape.45.gain_ref), custom_call_target="tpu_custom_call" | custom-call | tf_op jit(solution)/shard_map/pallas_call | solution.py:199
  76.7 0.3 copy.11
  77.0 2.3 %collective-permute-start.3 = (bf16[128,2240]{0,1:T(8,128)(2,1)S(1)}, bf16[128,2240]{0,1:T(8,128)(2,1)S(1)}, u32[]{:S(2)}, u32[]{:S(2)}) collective-permute-start(bf16[128,2240]{0,1:T(8,128)(2,1)S(1)} %copy.11), channel_id=1, source_target_pairs={{1,0},{2,1},{3,2},{4,3},{5,4},{6,5},{7,6},{8,7},{9,8},{10,9},{11,1... | collective-permute-start | bytes 1720328 | tf_op jit(solution)/shard_map/ppermute | solution.py:210
  79.3 1.0 %copy.10 = bf16[128,2240]{0,1:T(8,128)(2,1)} copy(bf16[128,2240]{1,0:T(8,128)(2,1)S(1)} %get-tuple-element.11.low_ref) | data formatting | bytes 1146880 | tf_op jit(solution)/shard_map/pallas_call | solution.py:199
  80.4 0.0 copy-start.3
  80.4 3.5 %collective-permute-start.2 = (bf16[128,2240]{0,1:T(8,128)(2,1)}, bf16[128,2240]{0,1:T(8,128)(2,1)S(1)}, u32[]{:S(2)}, u32[]{:S(2)}) collective-permute-start(bf16[128,2240]{0,1:T(8,128)(2,1)} %copy.10), channel_id=1, source_target_pairs={{0,1},{1,2},{2,3},{3,4},{4,5},{5,6},{6,7},{7,8},{8,9},{9,10},{10,1... | collective-permute-start | bytes 1720328 | tf_op jit(solution)/shard_map/ppermute | solution.py:209
  83.9 4.3 %collective-permute-done.3 = bf16[128,2240]{0,1:T(8,128)(2,1)S(1)} collective-permute-done((bf16[128,2240]{0,1:T(8,128)(2,1)S(1)}, bf16[128,2240]{0,1:T(8,128)(2,1)S(1)}, u32[]{:S(2)}, u32[]{:S(2)}) %collective-permute-start.3) | collective-permute-done | bytes 573472 | tf_op jit(solution)/shard_map/ppermute | solution.py:210
  88.2 0.2 copy.13.after_ref
  88.4 2.4 %collective-permute-done.2 = bf16[128,2240]{0,1:T(8,128)(2,1)S(1)} collective-permute-done((bf16[128,2240]{0,1:T(8,128)(2,1)}, bf16[128,2240]{0,1:T(8,128)(2,1)S(1)}, u32[]{:S(2)}, u32[]{:S(2)}) %collective-permute-start.2) | collective-permute-done | bytes 573472 | tf_op jit(solution)/shard_map/ppermute | solution.py:209
  90.8 0.2 copy.12.before_ref
  91.1 0.0 copy-done.3
  91.1 2.9 %shard_map.57 = bf16[256,2240]{1,0:T(8,128)(2,1)} custom-call(bf16[128,2240]{1,0:T(8,128)(2,1)S(1)} %copy.12.before_ref, bf16[128,2240]{1,0:T(8,128)(2,1)S(1)} %get-tuple-element.12.top_ref, bf16[128,2240]{1,0:T(8,128)(2,1)S(1)} %get-tuple-element.11.low_ref, bf16[128,2240]{1,0:T(8,128)(2,1)S(1)} %copy.13.after_ref, f32[9,2240]{1,0:T(8,128)S(1)} %copy-done.3), custom_call_target="tpu_custom_call" | custom-call | tf_op jit(solution)/shard_map/pallas_call | solution.py:211
  (7 shorter events, 0.1 us)
Async XLA Ops:
  0.0 1.3 %copy-start = (bf16[16,2,8,2240]{3,2,1,0:T(8,128)(2,1)S(1)}, bf16[16,2,8,2240]{3,2,1,0:T(8,128)(2,1)}, u32[]{:S(2)}) copy-start(bf16[16,2,8,2240]{3,2,1,0:T(8,128)(2,1)} %param.6) | copy-start | bytes 3440644
  1.3 1.3 %copy-start.1 = (bf16[16,2,8,2240]{3,2,1,0:T(8,128)(2,1)S(1)}, bf16[16,2,8,2240]{3,2,1,0:T(8,128)(2,1)}, u32[]{:S(2)}) copy-start(bf16[16,2,8,2240]{3,2,1,0:T(8,128)(2,1)} %param.7) | copy-start | bytes 3440644
  6.5 9.9 %collective-permute-start = (bf16[1024,128]{1,0:T(8,128)(2,1)S(1)}, bf16[1024,128]{1,0:T(8,128)(2,1)S(1)}, u32[]{:S(2)}, u32[]{:S(2)}) collective-permute-start(bf16[1024,128]{1,0:T(8,128)(2,1)S(1)} %get-tuple-element.10), channel_id=1, source_target_pairs={{0,1},{1,0},{2,3},{3,2},{4,5},{5,4},{6,7},{7,6},{8,9},{9,8},{10,11... | collective-permute-start | bytes 786440 | tf_op jit(solution)/shard_map/ppermute | solution.py:180
  30.3 43.6 %copy-start.4 = (f32[2240]{0:T(1024)S(1)}, f32[2240]{0:T(1024)}, u32[]{:S(2)}) copy-start(f32[2240]{0:T(1024)} %param.8) | copy-start | bytes 26884
  30.3 44.7 %copy-start.2 = (bf16[16,2,8,2240]{3,2,1,0:T(8,128)(2,1)S(1)}, bf16[16,2,8,2240]{3,2,1,0:T(8,128)(2,1)}, u32[]{:S(2)}) copy-start(bf16[16,2,8,2240]{3,2,1,0:T(8,128)(2,1)} %param.5) | copy-start | bytes 3440644
  31.1 19.4 %all-to-all-start.1 = ((bf16[8,4,32,128]{3,2,1,0:T(8,128)(2,1)}), bf16[8,4,32,128]{3,2,1,0:T(8,128)(2,1)S(1)}, u32[]{:S(2)}, u32[]{:S(2)}) async-start(bf16[8,4,32,128]{3,2,1,0:T(8,128)(2,1)} %broadcast_in_dim.4), calls=%async_computation.1 | async-start | bytes 524288 | tf_op jit(solution)/shard_map/all_to_all | solution.py:185
  67.6 7.4 %collective-permute-start.1 = (bf16[1024,128]{1,0:T(8,128)(2,1)S(1)}, bf16[1024,128]{1,0:T(8,128)(2,1)S(1)}, u32[]{:S(2)}, u32[]{:S(2)}) collective-permute-start(bf16[1024,128]{1,0:T(8,128)(2,1)S(1)} %bitcast.13), channel_id=1, source_target_pairs={{0,1},{1,0},{2,3},{3,2},{4,5},{5,4},{6,7},{7,6},{8,9},{9,8},{10,11... | collective-permute-start | bytes 786440 | tf_op jit(solution)/shard_map/ppermute | solution.py:197
  77.0 11.1 %collective-permute-start.3 = (bf16[128,2240]{0,1:T(8,128)(2,1)S(1)}, bf16[128,2240]{0,1:T(8,128)(2,1)S(1)}, u32[]{:S(2)}, u32[]{:S(2)}) collective-permute-start(bf16[128,2240]{0,1:T(8,128)(2,1)S(1)} %copy.11), channel_id=1, source_target_pairs={{1,0},{2,1},{3,2},{4,3},{5,4},{6,5},{7,6},{8,7},{9,8},{10,9},{11,1... | collective-permute-start | bytes 1720328 | tf_op jit(solution)/shard_map/ppermute | solution.py:210
  80.4 10.7 %copy-start.3 = (f32[9,2240]{1,0:T(8,128)S(1)}, f32[9,2240]{1,0:T(8,128)}, u32[]{:S(2)}) copy-start(f32[9,2240]{1,0:T(8,128)} %weight_ref.1) | copy-start | bytes 241924
  80.4 10.5 %collective-permute-start.2 = (bf16[128,2240]{0,1:T(8,128)(2,1)}, bf16[128,2240]{0,1:T(8,128)(2,1)S(1)}, u32[]{:S(2)}, u32[]{:S(2)}) collective-permute-start(bf16[128,2240]{0,1:T(8,128)(2,1)} %copy.10), channel_id=1, source_target_pairs={{0,1},{1,2},{2,3},{3,4},{4,5},{5,6},{6,7},{7,8},{8,9},{9,10},{10,1... | collective-permute-start | bytes 1720328 | tf_op jit(solution)/shard_map/ppermute | solution.py:209

commit v2 on v1

v2 whole, which is shorter than its diff:
```python
import jax
import jax.numpy as jnp
from jax import lax
from jax.experimental import pallas as pl
from jax.experimental.pallas import tpu as pltpu
from jax.sharding import Mesh, PartitionSpec as P

HEAD = 112
WIDTH = 2240
HEADS = WIDTH // HEAD
LANES = 128
TILES = 18
HALF_TILES = TILES // 2
PREFIX_FLOPS = 100_000_000
STATE_VMEM = 55_200_000
CHUNKS = 4
HALF_ROWS = 1024
EPS = 1e-06
F32, BF16 = jnp.float32, jnp.bfloat16
VMEM_LIMIT = 48 * 1024 * 1024


def tile_heads(tile):
    first = tile + tile // 7
    return first, HEAD * (first + 1) - LANES * tile


def lane_range(tile):
    return LANES * tile, min(LANES * (tile + 1), WIDTH)


def state_kernel(core_ref, k_ref, v_ref, mine_ref, other_ref, k_buf, v_buf, kt_ref, sems):
    core = core_ref[0]
    tokens = k_buf.shape[0]
    rows = tokens // CHUNKS
    copies = []
    for which, (ref, buf) in enumerate(((k_ref, k_buf), (v_ref, v_buf))):
        for chunk in range(CHUNKS):
            part = slice(rows * chunk, rows * (chunk + 1))
            copies.append(pltpu.make_async_copy(ref.at[part], buf.at[part], sems.at[which, chunk]))
    for copy in copies:
        copy.start()
    for copy in copies[:CHUNKS]:
        copy.wait()
    for tile in range(TILES):
        low, high = lane_range(tile)
        kt_ref[low:high, :] = jnp.maximum(k_buf[:, low:high], 0).T
    for copy in copies[CHUNKS:]:
        copy.wait()
    lane = lax.broadcasted_iota(jnp.int32, (HEAD, LANES), 1)
    ones = jnp.ones((tokens, LANES), BF16)
    for tile in range(TILES):
        first, end = tile_heads(tile)
        low, high = lane_range(tile)
        v = v_buf[:, low:high]
        if tile < TILES - 1:
            pair = jnp.dot(kt_ref[HEAD * first : HEAD * (first + 2), :], v, preferred_element_type=F32)
            state = jnp.where(lane < end, pair[:HEAD], pair[HEAD:])
        else:
            v = jnp.concatenate([v, jnp.zeros((tokens, LANES - v.shape[1]), BF16)], axis=1)
            state = jnp.dot(kt_ref[HEAD * first : WIDTH, :], v, preferred_element_type=F32)
            for head in range(HEADS):
                ksum = jnp.dot(
                    kt_ref[HEAD * head : HEAD * (head + 1), :], ones, preferred_element_type=F32
                )
                state = jnp.where(lane == end + head, ksum, state)
        half, place = divmod(tile, HALF_TILES)
        part = slice(HEAD * place, HEAD * (place + 1))

        @pl.when(core == half)
        def _():
            mine_ref[part, :] = state

        @pl.when(core != half)
        def _():
            other_ref[part, :] = state.astype(BF16)

    rest = slice(HEAD * HALF_TILES, HALF_ROWS)
    mine_ref[rest, :] = jnp.zeros((HALF_ROWS - HEAD * HALF_TILES, LANES), F32)
    other_ref[rest, :] = jnp.zeros((HALF_ROWS - HEAD * HALF_TILES, LANES), BF16)


def totals_kernel(pieces_ref, out_ref):
    zs, xs = out_ref.shape[:2]
    ys = pieces_ref.shape[0] // xs
    for x in range(xs):
        total = pieces_ref[ys * x].astype(F32)
        for y in range(1, ys):
            total = total + pieces_ref[ys * x + y].astype(F32)
        total = total.astype(BF16)
        for z in range(zs):
            out_ref[z, x] = total


def prefix_kernel(place_ref, blocks_ref, out_ref):
    zs, xs = blocks_ref.shape[:2]
    ys = out_ref.shape[0] // xs
    place = place_ref[0]
    before = jnp.zeros(blocks_ref.shape[2:], F32)
    for x in range(xs):
        upto, whole = before, before
        for z in range(zs):
            block = blocks_ref[z, x].astype(F32)
            upto = upto + jnp.where(z <= place, block, 0.0)
            whole = whole + block
        state = upto.astype(BF16)
        for y in range(ys):
            out_ref[ys * x + y] = state
        before = whole


def border_kernel(q_ref, top_ref, low_ref):
    tokens = q_ref.shape[0]
    for tile in range(TILES):
        low, high = lane_range(tile)
        wide = high - low
        q = jnp.maximum(q_ref[:, low:high], 0).astype(F32).reshape(tokens // 16, 2, 8, wide)
        top_ref[:, low:high] = q[:, 0].reshape(tokens // 2, wide).astype(BF16)
        low_ref[:, low:high] = q[:, 1].reshape(tokens // 2, wide).astype(BF16)
    rest = (tokens // 2, TILES * LANES - WIDTH)
    top_ref[:, WIDTH:] = jnp.zeros(rest, BF16)
    low_ref[:, WIDTH:] = jnp.zeros(rest, BF16)


def readout_kernel(
    core_ref, before_ref, q_ref, after_ref, mine_ref, other_ref, gain_ref, weight_ref, out_ref,
    state_ref, own_attn, before_attn, after_attn, own_scale, before_scale, after_scale, taps, out_buf, sems
):
    core = core_ref[0]
    tokens = q_ref.shape[0]
    state_ref[core] = mine_ref[...]
    state_ref[1 - core] = other_ref[...]
    lane = lax.broadcasted_iota(jnp.int32, (HEAD, LANES), 1)
    zero = jnp.zeros((HEAD, LANES), BF16)

    def tile_state(tile):
        half, place = divmod(tile, HALF_TILES)
        return state_ref[half, HEAD * place : HEAD * (place + 1), :]

    groups = (
        (q_ref, own_attn, own_scale),
        (before_ref, before_attn, before_scale),
        (after_ref, after_attn, after_scale),
    )
    last = tile_state(TILES - 1)
    last_end = tile_heads(TILES - 1)[1]
    squares = [jnp.zeros((group[0].shape[0], LANES), F32) for group in groups]
    for tile in range(TILES):
        first, end = tile_heads(tile)
        heads = [h for h in (first, first + 1) if h < HEADS]
        state = tile_state(tile)
        start = HEAD * first // LANES * LANES
        stop = min(start + 3 * LANES, WIDTH)
        parts = []
        offset = HEAD * first - start
        if offset:
            parts.append(jnp.zeros((offset, 2 * LANES), BF16))
        for position, head in enumerate(heads):
            inside = (lane < end) if position == 0 else (lane >= end)
            ksum = jnp.broadcast_to(last[:, last_end + head : last_end + head + 1], (HEAD, LANES))
            parts.append(
                jnp.concatenate([jnp.where(inside, state, zero), jnp.where(inside, ksum, zero)], axis=1)
            )
        remain = stop - start - offset - HEAD * len(heads)
        if remain:
            parts.append(jnp.zeros((remain, 2 * LANES), BF16))
        weights = jnp.concatenate(parts, axis=0)
        for place, (ref, attn_ref, _) in enumerate(groups):
            q = jnp.maximum(ref[:, start:stop], 0)
            both = jnp.dot(q, weights, preferred_element_type=F32)
            attn = both[:, :LANES] / (both[:, LANES:] + EPS)
            if tile == TILES - 1:
                keep = lax.broadcasted_iota(jnp.int32, attn.shape, 1) < end
                attn = jnp.where(keep, attn, 0.0)
            attn_ref[:, LANES * tile : LANES * (tile + 1)] = attn
            squares[place] = squares[place] + attn * attn
    for square, (_, _, scale_ref) in zip(squares, groups):
        mean = jnp.sum(square, axis=1, keepdims=True) * (1.0 / WIDTH)
        scale_ref[...] = jnp.broadcast_to(lax.rsqrt(mean + 1e-06), scale_ref.shape)

    for tile in range(TILES):
        low, high = lane_range(tile)
        col = lax.broadcasted_iota(jnp.int32, (8, high - low), 0)
        for tap in range(9):
            weight = jnp.broadcast_to(weight_ref[tap : tap + 1, low:high], (8, high - low))
            if tap % 3 == 0:
                weight = jnp.where(col == 0, 0.0, weight)
            if tap % 3 == 2:
                weight = jnp.where(col == 7, 0.0, weight)
            taps[tap, :, low:high] = weight

    rows = tokens // CHUNKS
    frames = rows // 16

    def one_chunk(chunk, carry):
        own = pl.ds(pl.multiple_of(chunk * rows, rows), rows)
        side = pl.ds(pl.multiple_of(chunk * (rows // 2), rows // 2), rows // 2)
        for tile in range(TILES):
            low, high = lane_range(tile)
            wide = high - low
            gain = gain_ref[:, low:high]

            def normed(attn_ref, scale_ref, part):
                value = attn_ref[part, low:high] * scale_ref[part, :wide] * gain
                return value.astype(BF16).astype(F32)

            own_rows = normed(own_attn, own_scale, own).reshape(frames, 2, 8, wide)
            four = (
                normed(before_attn, before_scale, side).reshape(frames, 8, wide),
                own_rows[:, 0],
                own_rows[:, 1],
                normed(after_attn, after_scale, side).reshape(frames, 8, wide),
            )
            totals = [None, None]
            for place, row in enumerate(four):
                moved = (pltpu.roll(row, 1, 1), row, pltpu.roll(row, 7, 1))
                for out_row in range(2):
                    row_off = place - out_row
                    if 0 <= row_off <= 2:
                        for col_off in range(3):
                            term = moved[col_off] * taps[3 * row_off + col_off, :, low:high][None]
                            totals[out_row] = term if totals[out_row] is None else totals[out_row] + term
            both = jnp.concatenate([totals[0][:, None], totals[1][:, None]], axis=1)
            out_buf[own, low:high] = both.reshape(rows, wide).astype(BF16)
        pltpu.make_async_copy(out_buf.at[own], out_ref.at[own], sems.at[chunk]).start()
        return carry

    lax.fori_loop(0, CHUNKS, one_chunk, 0)
    for chunk in range(CHUNKS):
        part = slice(rows * chunk, rows * (chunk + 1))
        pltpu.make_async_copy(out_buf.at[part], out_ref.at[part], sems.at[chunk]).wait()


def call(kernel, outs, in_specs, out_specs, scratch=(), flops=1_000_000_000, vmem=VMEM_LIMIT):
    return pl.pallas_call(
        kernel,
        out_shape=outs,
        in_specs=in_specs,
        out_specs=out_specs,
        scratch_shapes=scratch,
        compiler_params=pltpu.CompilerParams(vmem_limit_bytes=vmem),
        cost_estimate=pl.CostEstimate(flops=flops, bytes_accessed=5_000_000, transcendentals=0),
    )


VM = pl.BlockSpec(memory_space=pltpu.VMEM)
SM = pl.BlockSpec(memory_space=pltpu.SMEM)
HB = pl.BlockSpec(memory_space=pltpu.HBM)


def shards(queries, keys, values, gain, conv_weight):
    frames, rows, cols, width = queries.shape
    tokens = frames * rows * cols
    shape = jax.ShapeDtypeStruct
    core = lax.axis_index("core").reshape(1).astype(jnp.int32)
    swap = [(0, 1), (1, 0)]

    mine, other = call(
        state_kernel,
        [shape((HALF_ROWS, LANES), F32), shape((HALF_ROWS, LANES), BF16)],
        [SM, HB, HB],
        [VM, VM],
        [
            pltpu.VMEM((tokens, width), BF16),
            pltpu.VMEM((tokens, width), BF16),
            pltpu.VMEM((width, tokens), BF16),
            pltpu.SemaphoreType.DMA((2, CHUNKS)),
        ],
        vmem=STATE_VMEM,
    )(core, keys.reshape(tokens, width), values.reshape(tokens, width))

    xs, ys, zs = lax.axis_size("x"), lax.axis_size("y"), lax.axis_size("z")
    chunk = HALF_ROWS // (xs * ys)
    half = (mine + lax.ppermute(other, "core", swap).astype(F32)).astype(BF16)
    pieces = lax.all_to_all(half.reshape(xs * ys, chunk, LANES), ("x", "y"), 0, 0, tiled=True)
    totals = call(totals_kernel, shape((zs, xs, chunk, LANES), BF16), [VM], VM)(pieces)

    totals, q_late = lax.optimization_barrier((totals, queries.reshape(tokens, width)))
    border = shape((tokens // 2, TILES * LANES), BF16)
    top, low = call(border_kernel, [border] * 2, [VM], [VM] * 2, flops=20_000_000_000)(q_late)
    size = ys * 2
    up = [(i, i + 1) for i in range(size - 1)]
    down = [(i + 1, i) for i in range(size - 1)]
    q_before = lax.ppermute(low, ("y", "core"), up)
    q_after = lax.ppermute(top, ("y", "core"), down)

    blocks = lax.all_to_all(totals, "z", 0, 0, tiled=True)
    place = lax.axis_index("z").reshape(1).astype(jnp.int32)
    prefix = call(prefix_kernel, shape((xs * ys, chunk, LANES), BF16), [SM, VM], VM, flops=PREFIX_FLOPS)(place, blocks)
    held = lax.all_to_all(prefix, ("x", "y"), 0, 0, tiled=True)
    held, q_before, q_after = lax.optimization_barrier((held.reshape(HALF_ROWS, LANES), q_before, q_after))
    taken = lax.ppermute(held, "core", swap)

    padded = TILES * LANES
    out = call(
        readout_kernel,
        shape((tokens, width), BF16),
        [SM] + [VM] * 7,
        HB,
        [
            pltpu.VMEM((2, HALF_ROWS, LANES), BF16),
            pltpu.VMEM((tokens, padded), F32),
            pltpu.VMEM((tokens // 2, padded), F32),
            pltpu.VMEM((tokens // 2, padded), F32),
            pltpu.VMEM((tokens, LANES), F32),
            pltpu.VMEM((tokens // 2, LANES), F32),
            pltpu.VMEM((tokens // 2, LANES), F32),
            pltpu.VMEM((9, 8, padded), F32),
            pltpu.VMEM((tokens, width), BF16),
            pltpu.SemaphoreType.DMA((CHUNKS,)),
        ],
    )(
        core, q_before, queries.reshape(tokens, width), q_after, held, taken,
        gain.reshape(1, width), conv_weight,
    )
    return out.reshape(frames, rows, cols, width)


def solution(mesh):
    fine = Mesh(mesh.devices.reshape(4, 8, 8, 2), ("x", "z", "y", "core"))
    tokens = P(("x", "z"), ("y", "core"), None, None)
    return jax.shard_map(
        shards, mesh=fine, in_specs=(tokens, tokens, tokens, P(), P()), out_specs=tokens, check_vma=False
    )
```

time: 94.4 us -> 80.7 us (0.85)
  blocking collectives: 30.7 us -> 13.8 us
  starting transfers between devices: 30.8 us -> 40.8 us
  waiting for transfers between devices: 18.3 us -> 11.9 us
  local copies, waits for them, and re-layouts: 5.21 us -> 0.02 us
  Pallas kernels: 8.51 us -> 13.7 us
    all_to_all x1 -> x0, blocking collectives: 16.9 us -> none  [shards(): lax.all_to_all(prefix.reshape(xs * ys, chunk, LANES), ('x', 'y'), 0, 0, t...]
    all_to_all x1 -> x2, starting transfers between devices: 10 us -> 16.6 us  [the longest x1 10 us: shards(): blocks = lax.all_to_all(totals, 'z', 0, 0, tiled=True)]
    ppermute x2, waiting for transfers between devices: 6.7 us -> 1.92 us  [the longest x1 1.92 us: shards(): q_after = lax.ppermute(top, ('y', 'core'), down)]
    pallas_call x2 -> x4, Pallas kernels: 4.56 us -> 8.24 us  [the longest x1 5.63 us: shards(): call(readout_kernel, shape((tokens, width), BF16), [SM] + [VM] * 7, HB, [...]
    ppermute x2, starting transfers between devices: 5.78 us -> 9.19 us  [the longest x1 7.27 us: shards(): q_before = lax.ppermute(low, ('y', 'core'), up)]
    unnamed x10 -> x6, local copies, waits for them, and re-layouts: 2.56 us -> 0.01 us
    all_to_all x1 -> x2, waiting for transfers between devices: 9.37 us -> 7.73 us  [the longest x1 7.73 us: shards(): held = lax.all_to_all(prefix, ('x', 'y'), 0, 0, tiled=True)]
    pallas_call x1, Pallas kernels: 3.94 us -> 5.43 us  [shards(): call(state_kernel, [shape((HALF_ROWS, LANES), F32), shape((HALF_ROWS, LAN...]
  transfers between devices with their start and end apart: 5 -> 6, of which waited for: 5 -> 4; matrix products, arithmetic and copies ran while one was open for 1% -> 0% of each run, Pallas kernels for 0% -> 2%
where the time goes in v2:
time: 80.7 us; the launch traced here: 80.3 us
  starting transfers between devices  40.8 us (51%)
  blocking collectives  13.8 us (17%)
  Pallas kernels  13.7 us (17%)
  waiting for transfers between devices  11.9 us (15%)
    all_to_all x1, blocking collectives, shards(): lax.all_to_all(half.reshape(xs * ys, chunk, LANES), ('x', 'y'), 0, 0, til...  13.8 us
    all_to_all x1, starting transfers between devices, shards(): blocks = lax.all_to_all(totals, 'z', 0, 0, tiled=True)  10 us
    ppermute x1, starting transfers between devices, shards(): half = (mine + lax.ppermute(other, 'core', swap).astype(F32)).astype(BF16)  8.78 us
    all_to_all x1, waiting for transfers between devices, shards(): held = lax.all_to_all(prefix, ('x', 'y'), 0, 0, tiled=True)  7.73 us
    ppermute x1, starting transfers between devices, shards(): q_before = lax.ppermute(low, ('y', 'core'), up)  7.27 us
    all_to_all x1, starting transfers between devices, shards(): held = lax.all_to_all(prefix, ('x', 'y'), 0, 0, tiled=True)  6.54 us
    ppermute x1, starting transfers between devices, shards(): taken = lax.ppermute(held, 'core', swap)  6.21 us
    pallas_call x1, Pallas kernels, shards(): call(readout_kernel, shape((tokens, width), BF16), [SM] + [VM] * 7, HB, [...  5.63 us
  transfers between devices with their start and end apart: 6, of which 4 were waited for; matrix products, arithmetic and copies ran while one was open for 0% of the time, Pallas kernels for 2%

profile of v2, /device:TPU:1, one launch (start us, length us, event | category | flops | bytes accessed | tf_op | source)
XLA Modules:
  0.0 80.3 jit_solution(2207831807379269689)
XLA Ops:
  0.0 5.4 %shard_map.55 = (f32[1024,128]{1,0:T(8,128)S(1)}, bf16[1024,128]{1,0:T(8,128)(2,1)S(1)}) custom-call(s32[1]{0:T(128)} %bitcast.core_ref, bf16[256,2240]{1,0:T(8,128)(2,1)} %bitcast.13, bf16[256,2240]{1,0:T(8,128)(2,1)} %bitcast.14), custom_call_target="tpu_custom_call" | custom-call | flops 1000000000 | bytes 5000000 | tf_op jit(solution)/shard_map/pallas_call | solution.py:258
  5.4 8.8 %collective-permute-start = (bf16[1024,128]{1,0:T(8,128)(2,1)S(1)}, bf16[1024,128]{1,0:T(8,128)(2,1)S(1)}, u32[]{:S(2)}, u32[]{:S(2)}) collective-permute-start(bf16[1024,128]{1,0:T(8,128)(2,1)S(1)} %get-tuple-element.15), channel_id=1, source_target_pairs={{0,1},{1,0},{2,3},{3,2},{4,5},{5,4},{6,7},{7,6},{8,9},{9,8},{10,11... | collective-permute-start | bytes 786440 | tf_op jit(solution)/shard_map/ppermute | solution.py:274
  14.2 1.1 %collective-permute-done = bf16[1024,128]{1,0:T(8,128)(2,1)S(1)} collective-permute-done((bf16[1024,128]{1,0:T(8,128)(2,1)S(1)}, bf16[1024,128]{1,0:T(8,128)(2,1)S(1)}, u32[]{:S(2)}, u32[]{:S(2)}) %collective-permute-start) | collective-permute-done | bytes 262176 | tf_op jit(solution)/shard_map/ppermute | solution.py:274
  15.4 0.1 add_convert_fusion
  15.4 13.8 %all_to_all.15.pieces_ref = bf16[32,32,128]{2,1,0:T(8,128)(2,1)S(1)} all-to-all(bf16[32,32,128]{2,1,0:T(8,128)(2,1)S(1)} %bitcast.12), channel_id=1, replica_groups=mesh['x'=4,'z'=8,'y'=8,'core'=2] {'x','y'}, dimensions={0} | all-to-all | bytes 524288 | tf_op jit(solution)/shard_map/all_to_all | solution.py:275
  29.2 0.0 copy-start
  29.2 0.7 shard_map.56
  30.0 10.0 %all-to-all-start.1 = ((bf16[8,4,32,128]{3,2,1,0:T(8,128)(2,1)}), bf16[8,4,32,128]{3,2,1,0:T(8,128)(2,1)S(1)}, u32[]{:S(2)}, u32[]{:S(2)}) async-start(bf16[8,4,32,128]{3,2,1,0:T(8,128)(2,1)} %shard_map.56), calls=%async_computation.1 | async-start | bytes 524288 | tf_op jit(solution)/shard_map/all_to_all | solution.py:287
  40.0 0.0 copy-done
  40.0 0.0 copy-start.2
  40.0 1.1 %shard_map.58 = (bf16[128,2304]{1,0:T(8,128)(2,1)S(1)}, bf16[128,2304]{1,0:T(8,128)(2,1)}) custom-call(bf16[256,2240]{1,0:T(8,128)(2,1)S(1)} %bitcast.8), custom_call_target="tpu_custom_call" | custom-call | flops 20000000000 | bytes 5000000 | tf_op jit(solution)/shard_map/pallas_call | solution.py:280
  41.1 0.0 copy-start.1
  41.1 7.3 %collective-permute-start.1 = (bf16[128,2304]{1,0:T(8,128)(2,1)}, bf16[128,2304]{1,0:T(8,128)(2,1)S(1)}, u32[]{:S(2)}, u32[]{:S(2)}) collective-permute-start(bf16[128,2304]{1,0:T(8,128)(2,1)} %get-tuple-element.18), channel_id=1, source_target_pairs={{0,1},{1,2},{2,3},{3,4},{4,5},{5,6},{6,7},{7,8},{8,9},{9,10},{10,1... | collective-permute-start | bytes 1769480 | tf_op jit(solution)/shard_map/ppermute | solution.py:284
  48.4 1.9 %collective-permute-start.2 = (bf16[128,2304]{1,0:T(8,128)(2,1)S(1)}, bf16[128,2304]{1,0:T(8,128)(2,1)S(1)}, u32[]{:S(2)}, u32[]{:S(2)}) collective-permute-start(bf16[128,2304]{1,0:T(8,128)(2,1)S(1)} %get-tuple-element.19), channel_id=1, source_target_pairs={{1,0},{2,1},{3,2},{4,3},{5,4},{6,5},{7,6},{8,7},{9,8},{10,9},{11,1... | collective-permute-start | bytes 1769480 | tf_op jit(solution)/shard_map/ppermute | solution.py:285
  50.3 0.0 all-to-all-done.1.blocks_ref
  50.3 0.8 shard_map.57
  51.1 6.5 %all-to-all-start.2 = ((bf16[32,32,128]{2,1,0:T(8,128)(2,1)}), bf16[32,32,128]{2,1,0:T(8,128)(2,1)S(1)}, u32[]{:S(2)}, u32[]{:S(2)}) async-start(bf16[32,32,128]{2,1,0:T(8,128)(2,1)} %shard_map.57), calls=%async_computation.2 | async-start | bytes 524288 | tf_op jit(solution)/shard_map/all_to_all | solution.py:290
  57.6 0.0 collective-permute-done.1.before_ref
  57.7 1.9 %collective-permute-done.2.after_ref = bf16[128,2304]{1,0:T(8,128)(2,1)S(1)} collective-permute-done((bf16[128,2304]{1,0:T(8,128)(2,1)S(1)}, bf16[128,2304]{1,0:T(8,128)(2,1)S(1)}, u32[]{:S(2)}, u32[]{:S(2)}) %collective-permute-start.2) | collective-permute-done | bytes 589856 | tf_op jit(solution)/shard_map/ppermute | solution.py:285
  59.6 7.7 %all-to-all-done.2 = bf16[32,32,128]{2,1,0:T(8,128)(2,1)S(1)} async-done(((bf16[32,32,128]{2,1,0:T(8,128)(2,1)}), bf16[32,32,128]{2,1,0:T(8,128)(2,1)S(1)}, u32[]{:S(2)}, u32[]{:S(2)}) %all-to-all-start.2) | async-done | bytes 262176 | tf_op jit(solution)/shard_map/all_to_all | solution.py:290
  67.3 6.2 %collective-permute-start.3 = (bf16[1024,128]{1,0:T(8,128)(2,1)S(1)}, bf16[1024,128]{1,0:T(8,128)(2,1)S(1)}, u32[]{:S(2)}, u32[]{:S(2)}) collective-permute-start(bf16[1024,128]{1,0:T(8,128)(2,1)S(1)} %bitcast.10), channel_id=1, source_target_pairs={{0,1},{1,0},{2,3},{3,2},{4,5},{5,4},{6,7},{7,6},{8,9},{9,8},{10,11... | collective-permute-start | bytes 786440 | tf_op jit(solution)/shard_map/ppermute | solution.py:292
  73.5 0.0 copy-done.2
  73.5 1.1 %collective-permute-done.3.other_ref = bf16[1024,128]{1,0:T(8,128)(2,1)S(1)} collective-permute-done((bf16[1024,128]{1,0:T(8,128)(2,1)S(1)}, bf16[1024,128]{1,0:T(8,128)(2,1)S(1)}, u32[]{:S(2)}, u32[]{:S(2)}) %collective-permute-start.3) | collective-permute-done | bytes 262176 | tf_op jit(solution)/shard_map/ppermute | solution.py:292
  74.7 0.0 copy-done.1
  74.7 5.6 %shard_map.59 = bf16[256,2240]{1,0:T(8,128)(2,1)} custom-call(s32[1]{0:T(128)} %bitcast.core_ref, bf16[128,2304]{1,0:T(8,128)(2,1)S(1)} %collective-permute-done.1.before_ref, bf16[256,2240]{1,0:T(8,128)(2,1)S(1)} %bitcast.9, bf16[128,2304]{1,0:T(8,128)(2,1)S(1)} %collective-permute-done.2.after_ref, bf16[1024,128]{1,0:T(8,128)(2,1)S(1)} %bitcast.11, ...), custom_call_target="tpu_custom_call" | custom-call | flops 1000000000 | bytes 5000000 | tf_op jit(solution)/shard_map/pallas_call | solution.py:295
  (1 shorter events, 0.0 us)
Async XLA Ops:
  5.4 9.9 %collective-permute-start = (bf16[1024,128]{1,0:T(8,128)(2,1)S(1)}, bf16[1024,128]{1,0:T(8,128)(2,1)S(1)}, u32[]{:S(2)}, u32[]{:S(2)}) collective-permute-start(bf16[1024,128]{1,0:T(8,128)(2,1)S(1)} %get-tuple-element.15), channel_id=1, source_target_pairs={{0,1},{1,0},{2,3},{3,2},{4,5},{5,4},{6,7},{7,6},{8,9},{9,8},{10,11... | collective-permute-start | bytes 786440 | tf_op jit(solution)/shard_map/ppermute | solution.py:274
  29.2 10.8 %copy-start = (bf16[16,2,8,2240]{3,2,1,0:T(8,128)(2,1)S(1)}, bf16[16,2,8,2240]{3,2,1,0:T(8,128)(2,1)}, u32[]{:S(2)}) copy-start(bf16[16,2,8,2240]{3,2,1,0:T(8,128)(2,1)} %param.5) | copy-start | bytes 3440644
  30.0 20.3 %all-to-all-start.1 = ((bf16[8,4,32,128]{3,2,1,0:T(8,128)(2,1)}), bf16[8,4,32,128]{3,2,1,0:T(8,128)(2,1)S(1)}, u32[]{:S(2)}, u32[]{:S(2)}) async-start(bf16[8,4,32,128]{3,2,1,0:T(8,128)(2,1)} %shard_map.56), calls=%async_computation.1 | async-start | bytes 524288 | tf_op jit(solution)/shard_map/all_to_all | solution.py:287
  40.0 33.5 %copy-start.2 = (f32[2240]{0:T(1024)S(1)}, f32[2240]{0:T(1024)}, u32[]{:S(2)}) copy-start(f32[2240]{0:T(1024)} %param.8) | copy-start | bytes 26884
  41.1 33.6 %copy-start.1 = (f32[9,2240]{1,0:T(8,128)S(1)}, f32[9,2240]{1,0:T(8,128)}, u32[]{:S(2)}) copy-start(f32[9,2240]{1,0:T(8,128)} %weight_ref.1) | copy-start | bytes 241924
  41.1 16.6 %collective-permute-start.1 = (bf16[128,2304]{1,0:T(8,128)(2,1)}, bf16[128,2304]{1,0:T(8,128)(2,1)S(1)}, u32[]{:S(2)}, u32[]{:S(2)}) collective-permute-start(bf16[128,2304]{1,0:T(8,128)(2,1)} %get-tuple-element.18), channel_id=1, source_target_pairs={{0,1},{1,2},{2,3},{3,4},{4,5},{5,6},{6,7},{7,8},{8,9},{9,10},{10,1... | collective-permute-start | bytes 1769480 | tf_op jit(solution)/shard_map/ppermute | solution.py:284
  48.4 11.2 %collective-permute-start.2 = (bf16[128,2304]{1,0:T(8,128)(2,1)S(1)}, bf16[128,2304]{1,0:T(8,128)(2,1)S(1)}, u32[]{:S(2)}, u32[]{:S(2)}) collective-permute-start(bf16[128,2304]{1,0:T(8,128)(2,1)S(1)} %get-tuple-element.19), channel_id=1, source_target_pairs={{1,0},{2,1},{3,2},{4,3},{5,4},{6,5},{7,6},{8,7},{9,8},{10,9},{11,1... | collective-permute-start | bytes 1769480 | tf_op jit(solution)/shard_map/ppermute | solution.py:285
  51.1 16.2 %all-to-all-start.2 = ((bf16[32,32,128]{2,1,0:T(8,128)(2,1)}), bf16[32,32,128]{2,1,0:T(8,128)(2,1)S(1)}, u32[]{:S(2)}, u32[]{:S(2)}) async-start(bf16[32,32,128]{2,1,0:T(8,128)(2,1)} %shard_map.57), calls=%async_computation.2 | async-start | bytes 524288 | tf_op jit(solution)/shard_map/all_to_all | solution.py:290
  67.3 7.4 %collective-permute-start.3 = (bf16[1024,128]{1,0:T(8,128)(2,1)S(1)}, bf16[1024,128]{1,0:T(8,128)(2,1)S(1)}, u32[]{:S(2)}, u32[]{:S(2)}) collective-permute-start(bf16[1024,128]{1,0:T(8,128)(2,1)S(1)} %bitcast.10), channel_id=1, source_target_pairs={{0,1},{1,0},{2,3},{3,2},{4,5},{5,4},{6,7},{7,6},{8,9},{9,8},{10,11... | collective-permute-start | bytes 786440 | tf_op jit(solution)/shard_map/ppermute | solution.py:292

commit v3 on v2

--- a/solution.py
+++ b/solution.py
@@ -29,7 +29,7 @@
     return LANES * tile, min(LANES * (tile + 1), WIDTH)
 
 
-def state_kernel(core_ref, k_ref, v_ref, mine_ref, other_ref, k_buf, v_buf, kt_ref, sems):
+def state_kernel(core_ref, k_ref, v_ref, mine_ref, other_ref, k_buf, v_buf, kt_ref, state_ref, sems):
     core = core_ref[0]
     tokens = k_buf.shape[0]
     rows = tokens // CHUNKS
@@ -65,19 +65,12 @@
                 )
                 state = jnp.where(lane == end + head, ksum, state)
         half, place = divmod(tile, HALF_TILES)
-        part = slice(HEAD * place, HEAD * (place + 1))
-
-        @pl.when(core == half)
-        def _():
-            mine_ref[part, :] = state
-
-        @pl.when(core != half)
-        def _():
-            other_ref[part, :] = state.astype(BF16)
-
-    rest = slice(HEAD * HALF_TILES, HALF_ROWS)
-    mine_ref[rest, :] = jnp.zeros((HALF_ROWS - HEAD * HALF_TILES, LANES), F32)
-    other_ref[rest, :] = jnp.zeros((HALF_ROWS - HEAD * HALF_TILES, LANES), BF16)
+        state_ref[half, HEAD * place : HEAD * (place + 1), :] = state
+    rest = HEAD * HALF_TILES
+    mine_ref[:rest, :] = state_ref[core]
+    other_ref[:rest, :] = state_ref[1 - core].astype(BF16)
+    mine_ref[rest:, :] = jnp.zeros((HALF_ROWS - rest, LANES), F32)
+    other_ref[rest:, :] = jnp.zeros((HALF_ROWS - rest, LANES), BF16)
 
 
 def totals_kernel(pieces_ref, out_ref):
@@ -122,12 +115,25 @@
     low_ref[:, WIDTH:] = jnp.zeros(rest, BF16)
 
 
+def heads_kernel(q_ref, before_ref, after_ref, gain_ref, weight_ref, out_ref, rows_ref):
+    taps = weight_ref.shape[0]
+    rows_ref[:taps, :WIDTH] = weight_ref[...]
+    rows_ref[taps : taps + 1, :WIDTH] = gain_ref[...]
+    place = 0
+    for ref in (q_ref, before_ref, after_ref):
+        rows = ref.shape[0]
+        fill = jnp.zeros((rows, LANES - HEAD), BF16)
+        for head in range(HEADS):
+            q = jnp.maximum(ref[:, HEAD * head : HEAD * (head + 1)], 0)
+            out_ref[place : place + rows, LANES * head : LANES * (head + 1)] = jnp.concatenate([q, fill], axis=1)
+        place += rows
+
+
 def readout_kernel(
-    core_ref, before_ref, q_ref, after_ref, mine_ref, other_ref, gain_ref, weight_ref, out_ref,
-    state_ref, own_attn, before_attn, after_attn, own_scale, before_scale, after_scale, taps, out_buf, sems
+    core_ref, q_ref, mine_ref, other_ref, rows_ref, out_ref, state_ref, attn_ref, scale_ref, taps, out_buf, sems
 ):
     core = core_ref[0]
-    tokens = q_ref.shape[0]
+    tokens = q_ref.shape[0] // 2
     state_ref[core] = mine_ref[...]
     state_ref[1 - core] = other_ref[...]
     lane = lax.broadcasted_iota(jnp.int32, (HEAD, LANES), 1)
@@ -137,56 +143,44 @@
         half, place = divmod(tile, HALF_TILES)
         return state_ref[half, HEAD * place : HEAD * (place + 1), :]
 
-    groups = (
-        (q_ref, own_attn, own_scale),
-        (before_ref, before_attn, before_scale),
-        (after_ref, after_attn, after_scale),
-    )
     last = tile_state(TILES - 1)
     last_end = tile_heads(TILES - 1)[1]
-    squares = [jnp.zeros((group[0].shape[0], LANES), F32) for group in groups]
+    square = jnp.zeros((2 * tokens, LANES), F32)
+    fill = jnp.zeros((LANES - HEAD, 2 * LANES), BF16)
     for tile in range(TILES):
         first, end = tile_heads(tile)
         heads = [h for h in (first, first + 1) if h < HEADS]
         state = tile_state(tile)
-        start = HEAD * first // LANES * LANES
-        stop = min(start + 3 * LANES, WIDTH)
         parts = []
-        offset = HEAD * first - start
-        if offset:
-            parts.append(jnp.zeros((offset, 2 * LANES), BF16))
         for position, head in enumerate(heads):
             inside = (lane < end) if position == 0 else (lane >= end)
             ksum = jnp.broadcast_to(last[:, last_end + head : last_end + head + 1], (HEAD, LANES))
             parts.append(
                 jnp.concatenate([jnp.where(inside, state, zero), jnp.where(inside, ksum, zero)], axis=1)
             )
-        remain = stop - start - offset - HEAD * len(heads)
-        if remain:
-            parts.append(jnp.zeros((remain, 2 * LANES), BF16))
+            parts.append(fill)
         weights = jnp.concatenate(parts, axis=0)
-        for place, (ref, attn_ref, _) in enumerate(groups):
-            q = jnp.maximum(ref[:, start:stop], 0)
-            both = jnp.dot(q, weights, preferred_element_type=F32)
-            attn = both[:, :LANES] / (both[:, LANES:] + EPS)
-            if tile == TILES - 1:
-                keep = lax.broadcasted_iota(jnp.int32, attn.shape, 1) < end
-                attn = jnp.where(keep, attn, 0.0)
-            attn_ref[:, LANES * tile : LANES * (tile + 1)] = attn
-            squares[place] = squares[place] + attn * attn
-    for square, (_, _, scale_ref) in zip(squares, groups):
-        mean = jnp.sum(square, axis=1, keepdims=True) * (1.0 / WIDTH)
-        scale_ref[...] = jnp.broadcast_to(lax.rsqrt(mean + 1e-06), scale_ref.shape)
+        q = q_ref[:, LANES * first : LANES * (first + len(heads))]
+        both = jnp.dot(q, weights, preferred_element_type=F32)
+        attn = both[:, :LANES] / (both[:, LANES:] + EPS)
+        if tile == TILES - 1:
+            keep = lax.broadcasted_iota(jnp.int32, attn.shape, 1) < end
+            attn = jnp.where(keep, attn, 0.0)
+        square = square + attn * attn
+        low, high = lane_range(tile)
+        attn_ref[:, low:high] = attn[:, : high - low] * rows_ref[9:10, low:high]
+    mean = jnp.sum(square, axis=1, keepdims=True) * (1.0 / WIDTH)
+    scale_ref[...] = jnp.broadcast_to(lax.rsqrt(mean + 1e-06), scale_ref.shape)
 
     for tile in range(TILES):
         low, high = lane_range(tile)
         col = lax.broadcasted_iota(jnp.int32, (8, high - low), 0)
         for tap in range(9):
-            weight = jnp.broadcast_to(weight_ref[tap : tap + 1, low:high], (8, high - low))
+            weight = jnp.broadcast_to(rows_ref[tap : tap + 1, low:high], (8, high - low))
             if tap % 3 == 0:
+                weight = jnp.where(col == 7, 0.0, weight)
+            if tap % 3 == 2:
                 weight = jnp.where(col == 0, 0.0, weight)
-            if tap % 3 == 2:
-                weight = jnp.where(col == 7, 0.0, weight)
             taps[tap, :, low:high] = weight
 
     rows = tokens // CHUNKS
@@ -194,32 +188,28 @@
 
     def one_chunk(chunk, carry):
         own = pl.ds(pl.multiple_of(chunk * rows, rows), rows)
-        side = pl.ds(pl.multiple_of(chunk * (rows // 2), rows // 2), rows // 2)
+        before = pl.ds(pl.multiple_of(tokens + chunk * (rows // 2), rows // 2), rows // 2)
+        after = pl.ds(pl.multiple_of(tokens + tokens // 2 + chunk * (rows // 2), rows // 2), rows // 2)
         for tile in range(TILES):
             low, high = lane_range(tile)
             wide = high - low
-            gain = gain_ref[:, low:high]
-
-            def normed(attn_ref, scale_ref, part):
-                value = attn_ref[part, low:high] * scale_ref[part, :wide] * gain
-                return value.astype(BF16).astype(F32)
-
-            own_rows = normed(own_attn, own_scale, own).reshape(frames, 2, 8, wide)
-            four = (
-                normed(before_attn, before_scale, side).reshape(frames, 8, wide),
-                own_rows[:, 0],
-                own_rows[:, 1],
-                normed(after_attn, after_scale, side).reshape(frames, 8, wide),
-            )
-            totals = [None, None]
-            for place, row in enumerate(four):
-                moved = (pltpu.roll(row, 1, 1), row, pltpu.roll(row, 7, 1))
-                for out_row in range(2):
-                    row_off = place - out_row
-                    if 0 <= row_off <= 2:
-                        for col_off in range(3):
-                            term = moved[col_off] * taps[3 * row_off + col_off, :, low:high][None]
-                            totals[out_row] = term if totals[out_row] is None else totals[out_row] + term
+
+            def normed(part):
+                value = attn_ref[part, low:high] * scale_ref[part, :wide]
+                return value.astype(BF16).astype(F32).reshape(-1, 8, wide)
+
+            own_rows = normed(own).reshape(frames, 2, 8, wide)
+            four = (normed(before), own_rows[:, 0], own_rows[:, 1], normed(after))
+            totals = []
+            for out_row in range(2):
+                sums = []
+                for col_off in range(3):
+                    terms = [
+                        four[out_row + row_off] * taps[3 * row_off + col_off, :, low:high][None]
+                        for row_off in range(3)
+                    ]
+                    sums.append(terms[0] + terms[1] + terms[2])
+                totals.append(pltpu.roll(sums[0], 1, 1) + sums[1] + pltpu.roll(sums[2], 7, 1))
             both = jnp.concatenate([totals[0][:, None], totals[1][:, None]], axis=1)
             out_buf[own, low:high] = both.reshape(rows, wide).astype(BF16)
         pltpu.make_async_copy(out_buf.at[own], out_ref.at[own], sems.at[chunk]).start()
@@ -264,6 +254,7 @@
             pltpu.VMEM((tokens, width), BF16),
             pltpu.VMEM((tokens, width), BF16),
             pltpu.VMEM((width, tokens), BF16),
+            pltpu.VMEM((2, HEAD * HALF_TILES, LANES), F32),
             pltpu.SemaphoreType.DMA((2, CHUNKS)),
         ],
         vmem=STATE_VMEM,
@@ -288,31 +279,30 @@
     place = lax.axis_index("z").reshape(1).astype(jnp.int32)
     prefix = call(prefix_kernel, shape((xs * ys, chunk, LANES), BF16), [SM, VM], VM, flops=PREFIX_FLOPS)(place, blocks)
     held = lax.all_to_all(prefix, ("x", "y"), 0, 0, tiled=True)
-    held, q_before, q_after = lax.optimization_barrier((held.reshape(HALF_ROWS, LANES), q_before, q_after))
+    by_head, taps = call(
+        heads_kernel,
+        [shape((2 * tokens, HEADS * LANES), BF16), shape((16, TILES * LANES), F32)],
+        [VM] * 5,
+        [VM] * 2,
+    )(q_late, q_before, q_after, gain.reshape(1, width), conv_weight)
+    held, by_head, taps = lax.optimization_barrier((held.reshape(HALF_ROWS, LANES), by_head, taps))
     taken = lax.ppermute(held, "core", swap)
 
     padded = TILES * LANES
     out = call(
         readout_kernel,
         shape((tokens, width), BF16),
-        [SM] + [VM] * 7,
+        [SM] + [VM] * 4,
         HB,
         [
             pltpu.VMEM((2, HALF_ROWS, LANES), BF16),
-            pltpu.VMEM((tokens, padded), F32),
-            pltpu.VMEM((tokens // 2, padded), F32),
-            pltpu.VMEM((tokens // 2, padded), F32),
-            pltpu.VMEM((tokens, LANES), F32),
-            pltpu.VMEM((tokens // 2, LANES), F32),
-            pltpu.VMEM((tokens // 2, LANES), F32),
+            pltpu.VMEM((2 * tokens, padded), F32),
+            pltpu.VMEM((2 * tokens, LANES), F32),
             pltpu.VMEM((9, 8, padded), F32),
             pltpu.VMEM((tokens, width), BF16),
             pltpu.SemaphoreType.DMA((CHUNKS,)),
         ],
-    )(
-        core, q_before, queries.reshape(tokens, width), q_after, held, taken,
-        gain.reshape(1, width), conv_weight,
-    )
+    )(core, by_head, held, taken, taps)
     return out.reshape(frames, rows, cols, width)
 
 

time: 80.7 us -> 76.8 us (0.952)
  waiting for transfers between devices: 11.9 us -> 5.65 us
  local copies, waits for them, and re-layouts: 0.02 us -> 5.06 us
  Pallas kernels: 13.7 us -> 10 us
    unnamed x6 -> x16, local copies, waits for them, and re-layouts: 0.01 us -> 5.05 us
    all_to_all x1, waiting for transfers between devices: 7.73 us -> 3.19 us  [shards(): held = lax.all_to_all(prefix, ('x', 'y'), 0, 0, tiled=True)]
    pallas_call x1, Pallas kernels: 5.43 us -> 2.68 us  [shards(): call(state_kernel, [shape((HALF_ROWS, LANES), F32), shape((HALF_ROWS, LAN...]
    ppermute x1, waiting for transfers between devices: 1.92 us -> 0.18 us  [shards(): q_after = lax.ppermute(top, ('y', 'core'), down)]
    all_to_all x1, starting transfers between devices: 6.54 us -> 7.45 us  [shards(): held = lax.all_to_all(prefix, ('x', 'y'), 0, 0, tiled=True)]
    pallas_call x1 -> x2, Pallas kernels: 5.63 us -> 5.53 us  [the longest x1 4.34 us: shards(): call(readout_kernel, shape((tokens, width), BF16), [SM] + [VM] * 4, HB, [...]
  transfers between devices with their start and end apart: 6 -> 6, of which waited for: 4 -> 4; matrix products, arithmetic and copies ran while one was open for 0% -> 0% of each run, Pallas kernels for 2% -> 3%
where the time goes in v3:
time: 76.8 us; the launch traced here: 76.2 us
  starting transfers between devices  41.5 us (54%)
  blocking collectives  13.8 us (18%)
  Pallas kernels  10 us (13%)
  waiting for transfers between devices  5.65 us (7%)
  local copies, waits for them, and re-layouts  5.06 us (7%)
    all_to_all x1, blocking collectives, shards(): lax.all_to_all(half.reshape(xs * ys, chunk, LANES), ('x', 'y'), 0, 0, til...  13.8 us
    all_to_all x1, starting transfers between devices, shards(): blocks = lax.all_to_all(totals, 'z', 0, 0, tiled=True)  10 us
    ppermute x1, starting transfers between devices, shards(): half = (mine + lax.ppermute(other, 'core', swap).astype(F32)).astype(BF16)  8.79 us
    all_to_all x1, starting transfers between devices, shards(): held = lax.all_to_all(prefix, ('x', 'y'), 0, 0, tiled=True)  7.45 us
    ppermute x1, starting transfers between devices, shards(): q_before = lax.ppermute(low, ('y', 'core'), up)  7.15 us
    ppermute x1, starting transfers between devices, shards(): taken = lax.ppermute(held, 'core', swap)  6.21 us
    unnamed x16, local copies, waits for them, and re-layouts  5.05 us
    pallas_call x1, Pallas kernels, shards(): call(readout_kernel, shape((tokens, width), BF16), [SM] + [VM] * 4, HB, [...  4.34 us
  transfers between devices with their start and end apart: 6, of which 4 were waited for; matrix products, arithmetic and copies ran while one was open for 0% of the time, Pallas kernels for 3%

profile of v3, /device:TPU:1, one launch (start us, length us, event | category | flops | bytes accessed | tf_op | source)
XLA Modules:
  0.0 76.2 jit_solution(10245869411093413076)
XLA Ops:
  0.0 2.7 %shard_map.55 = (f32[1024,128]{1,0:T(8,128)S(1)}, bf16[1024,128]{1,0:T(8,128)(2,1)S(1)}) custom-call(s32[1]{0:T(128)} %bitcast.core_ref, bf16[256,2240]{1,0:T(8,128)(2,1)} %bitcast.13, bf16[256,2240]{1,0:T(8,128)(2,1)} %bitcast.14), custom_call_target="tpu_custom_call" | custom-call | flops 1000000000 | bytes 5000000 | tf_op jit(solution)/shard_map/pallas_call | solution.py:248
  2.7 8.8 %collective-permute-start = (bf16[1024,128]{1,0:T(8,128)(2,1)S(1)}, bf16[1024,128]{1,0:T(8,128)(2,1)S(1)}, u32[]{:S(2)}, u32[]{:S(2)}) collective-permute-start(bf16[1024,128]{1,0:T(8,128)(2,1)S(1)} %get-tuple-element.17), channel_id=1, source_target_pairs={{0,1},{1,0},{2,3},{3,2},{4,5},{5,4},{6,7},{7,6},{8,9},{9,8},{10,11... | collective-permute-start | bytes 786440 | tf_op jit(solution)/shard_map/ppermute | solution.py:265
  11.5 1.1 %collective-permute-done = bf16[1024,128]{1,0:T(8,128)(2,1)S(1)} collective-permute-done((bf16[1024,128]{1,0:T(8,128)(2,1)S(1)}, bf16[1024,128]{1,0:T(8,128)(2,1)S(1)}, u32[]{:S(2)}, u32[]{:S(2)}) %collective-permute-start) | collective-permute-done | bytes 262176 | tf_op jit(solution)/shard_map/ppermute | solution.py:265
  12.6 0.1 add_convert_fusion
  12.7 13.8 %all_to_all.15.pieces_ref = bf16[32,32,128]{2,1,0:T(8,128)(2,1)S(1)} all-to-all(bf16[32,32,128]{2,1,0:T(8,128)(2,1)S(1)} %bitcast.12), channel_id=1, replica_groups=mesh['x'=4,'z'=8,'y'=8,'core'=2] {'x','y'}, dimensions={0} | all-to-all | bytes 524288 | tf_op jit(solution)/shard_map/all_to_all | solution.py:266
  26.5 0.0 copy-start
  26.5 0.7 shard_map.56
  27.2 10.0 %all-to-all-start.1 = ((bf16[8,4,32,128]{3,2,1,0:T(8,128)(2,1)}), bf16[8,4,32,128]{3,2,1,0:T(8,128)(2,1)S(1)}, u32[]{:S(2)}, u32[]{:S(2)}) async-start(bf16[8,4,32,128]{3,2,1,0:T(8,128)(2,1)} %shard_map.56), calls=%async_computation.1 | async-start | bytes 524288 | tf_op jit(solution)/shard_map/all_to_all | solution.py:278
  37.2 0.0 copy-done
  37.3 0.0 copy-start.7
  37.3 0.0 copy-start.6
  37.3 0.3 shard_map.58
  37.6 7.2 %collective-permute-start.1 = (bf16[128,2304]{1,0:T(8,128)(2,1)S(1)}, bf16[128,2304]{1,0:T(8,128)(2,1)S(1)}, u32[]{:S(2)}, u32[]{:S(2)}) collective-permute-start(bf16[128,2304]{1,0:T(8,128)(2,1)S(1)} %get-tuple-element.20), channel_id=1, source_target_pairs={{0,1},{1,2},{2,3},{3,4},{4,5},{5,6},{6,7},{7,8},{8,9},{9,10},{10,1... | collective-permute-start | bytes 1769480 | tf_op jit(solution)/shard_map/ppermute | solution.py:275
  44.7 1.9 %collective-permute-start.2 = (bf16[128,2304]{1,0:T(8,128)(2,1)S(1)}, bf16[128,2304]{1,0:T(8,128)(2,1)S(1)}, u32[]{:S(2)}, u32[]{:S(2)}) collective-permute-start(bf16[128,2304]{1,0:T(8,128)(2,1)S(1)} %get-tuple-element.21), channel_id=1, source_target_pairs={{1,0},{2,1},{3,2},{4,3},{5,4},{6,5},{7,6},{8,7},{9,8},{10,9},{11,1... | collective-permute-start | bytes 1769480 | tf_op jit(solution)/shard_map/ppermute | solution.py:276
  46.7 0.0 all-to-all-done.1.blocks_ref
  46.7 0.8 %shard_map.57 = bf16[32,32,128]{2,1,0:T(8,128)(2,1)} custom-call(s32[1]{0:T(128)} %bitcast.1.place_ref, bf16[8,4,32,128]{3,2,1,0:T(8,128)(2,1)S(1)} %all-to-all-done.1.blocks_ref), custom_call_target="tpu_custom_call" | custom-call | flops 100000000 | bytes 5000000 | tf_op jit(solution)/shard_map/pallas_call | solution.py:280
  47.4 7.4 %all-to-all-start.2 = ((bf16[32,32,128]{2,1,0:T(8,128)(2,1)}), bf16[32,32,128]{2,1,0:T(8,128)(2,1)S(1)}, u32[]{:S(2)}, u32[]{:S(2)}) async-start(bf16[32,32,128]{2,1,0:T(8,128)(2,1)} %shard_map.57), calls=%async_computation.2 | async-start | bytes 524288 | tf_op jit(solution)/shard_map/all_to_all | solution.py:281
  54.9 0.0 copy-done.7
  54.9 0.0 collective-permute-done.1.before_ref
  54.9 0.0 copy-start.2
  54.9 0.8 %copy-done.2 = bf16[128,2304]{1,0:T(8,128)(2,1)} copy-done((bf16[128,2304]{1,0:T(8,128)(2,1)}, bf16[128,2304]{1,0:T(8,128)(2,1)S(1)}, u32[]{:S(2)}) %copy-start.2) | copy-done | bytes 589848
  55.7 0.2 collective-permute-done.2.after_ref
  55.9 0.0 copy-start.4
  55.9 0.8 %copy-done.4 = bf16[128,2304]{1,0:T(8,128)(2,1)} copy-done((bf16[128,2304]{1,0:T(8,128)(2,1)}, bf16[128,2304]{1,0:T(8,128)(2,1)S(1)}, u32[]{:S(2)}) %copy-start.4) | copy-done | bytes 589848
  56.8 0.0 copy-done.6
  56.8 0.0 copy-start.1
  56.8 1.3 %copy-done.1 = bf16[16,2,8,2240]{3,2,1,0:T(8,128)(2,1)S(1)} copy-done((bf16[16,2,8,2240]{3,2,1,0:T(8,128)(2,1)S(1)}, bf16[16,2,8,2240]{3,2,1,0:T(8,128)(2,1)}, u32[]{:S(2)}) %copy-start.1) | copy-done | bytes 1146904
  58.0 0.0 copy-start.3
  58.0 1.1 %copy-done.3 = bf16[128,2304]{1,0:T(8,128)(2,1)S(1)} copy-done((bf16[128,2304]{1,0:T(8,128)(2,1)S(1)}, bf16[128,2304]{1,0:T(8,128)(2,1)}, u32[]{:S(2)}) %copy-start.3) | copy-done | bytes 589848
  59.1 0.0 copy-start.5
  59.1 1.1 %copy-done.5 = bf16[128,2304]{1,0:T(8,128)(2,1)S(1)} copy-done((bf16[128,2304]{1,0:T(8,128)(2,1)S(1)}, bf16[128,2304]{1,0:T(8,128)(2,1)}, u32[]{:S(2)}) %copy-start.5) | copy-done | bytes 589848
  60.2 1.2 %shard_map.59 = (bf16[512,2560]{1,0:T(8,128)(2,1)S(1)}, f32[16,2304]{1,0:T(8,128)S(1)}) custom-call(bf16[256,2240]{1,0:T(8,128)(2,1)S(1)} %bitcast.11, bf16[128,2304]{1,0:T(8,128)(2,1)S(1)} %copy-done.3, bf16[128,2304]{1,0:T(8,128)(2,1)S(1)} %copy-done.5, f32[1,2240]{1,0:T(1,128)S(1)} %reshape.34.gain_ref, f32[9,2240]{1,0:T(8,128)S(1)} %copy-done.6), custom_call_target="tpu_custom_call" | custom-call | flops 1000000000 | bytes 5000000 | tf_op jit(solution)/shard_map/pallas_call | solution.py:282
  61.4 3.2 %all-to-all-done.2 = bf16[32,32,128]{2,1,0:T(8,128)(2,1)S(1)} async-done(((bf16[32,32,128]{2,1,0:T(8,128)(2,1)}), bf16[32,32,128]{2,1,0:T(8,128)(2,1)S(1)}, u32[]{:S(2)}, u32[]{:S(2)}) %all-to-all-start.2) | async-done | bytes 262176 | tf_op jit(solution)/shard_map/all_to_all | solution.py:281
  64.5 6.2 %collective-permute-start.3 = (bf16[1024,128]{1,0:T(8,128)(2,1)S(1)}, bf16[1024,128]{1,0:T(8,128)(2,1)S(1)}, u32[]{:S(2)}, u32[]{:S(2)}) collective-permute-start(bf16[1024,128]{1,0:T(8,128)(2,1)S(1)} %bitcast.8), channel_id=1, source_target_pairs={{0,1},{1,0},{2,3},{3,2},{4,5},{5,4},{6,7},{7,6},{8,9},{9,8},{10,11... | collective-permute-start | bytes 786440 | tf_op jit(solution)/shard_map/ppermute | solution.py:289
  70.8 1.1 %collective-permute-done.3.other_ref = bf16[1024,128]{1,0:T(8,128)(2,1)S(1)} collective-permute-done((bf16[1024,128]{1,0:T(8,128)(2,1)S(1)}, bf16[1024,128]{1,0:T(8,128)(2,1)S(1)}, u32[]{:S(2)}, u32[]{:S(2)}) %collective-permute-start.3) | collective-permute-done | bytes 262176 | tf_op jit(solution)/shard_map/ppermute | solution.py:289
  71.9 4.3 %shard_map.60 = bf16[256,2240]{1,0:T(8,128)(2,1)} custom-call(s32[1]{0:T(128)} %bitcast.core_ref, bf16[512,2560]{1,0:T(8,128)(2,1)S(1)} %get-tuple-element.24.q_ref, bf16[1024,128]{1,0:T(8,128)(2,1)S(1)} %bitcast.9, bf16[1024,128]{1,0:T(8,128)(2,1)S(1)} %collective-permute-done.3.other_ref, f32[16,2304]{1,0:T(8,128)S(1)} %get-tuple-element.26.rows_ref), custom_call_target="tpu_custom_call" | custom-call | flops 1000000000 | bytes 5000000 | tf_op jit(solution)/shard_map/pallas_call | solution.py:292
  (1 shorter events, 0.0 us)
Async XLA Ops:
  2.7 9.9 %collective-permute-start = (bf16[1024,128]{1,0:T(8,128)(2,1)S(1)}, bf16[1024,128]{1,0:T(8,128)(2,1)S(1)}, u32[]{:S(2)}, u32[]{:S(2)}) collective-permute-start(bf16[1024,128]{1,0:T(8,128)(2,1)S(1)} %get-tuple-element.17), channel_id=1, source_target_pairs={{0,1},{1,0},{2,3},{3,2},{4,5},{5,4},{6,7},{7,6},{8,9},{9,8},{10,11... | collective-permute-start | bytes 786440 | tf_op jit(solution)/shard_map/ppermute | solution.py:265
  26.5 10.8 %copy-start = (bf16[16,2,8,2240]{3,2,1,0:T(8,128)(2,1)S(1)}, bf16[16,2,8,2240]{3,2,1,0:T(8,128)(2,1)}, u32[]{:S(2)}) copy-start(bf16[16,2,8,2240]{3,2,1,0:T(8,128)(2,1)} %param.5) | copy-start | bytes 3440644
  27.2 19.4 %all-to-all-start.1 = ((bf16[8,4,32,128]{3,2,1,0:T(8,128)(2,1)}), bf16[8,4,32,128]{3,2,1,0:T(8,128)(2,1)S(1)}, u32[]{:S(2)}, u32[]{:S(2)}) async-start(bf16[8,4,32,128]{3,2,1,0:T(8,128)(2,1)} %shard_map.56), calls=%async_computation.1 | async-start | bytes 524288 | tf_op jit(solution)/shard_map/all_to_all | solution.py:278
  37.3 17.6 %copy-start.7 = (f32[2240]{0:T(1024)S(1)}, f32[2240]{0:T(1024)}, u32[]{:S(2)}) copy-start(f32[2240]{0:T(1024)} %param.8) | copy-start | bytes 26884
  37.3 19.5 %copy-start.6 = (f32[9,2240]{1,0:T(8,128)S(1)}, f32[9,2240]{1,0:T(8,128)}, u32[]{:S(2)}) copy-start(f32[9,2240]{1,0:T(8,128)} %weight_ref.1) | copy-start | bytes 241924
  37.6 17.4 %collective-permute-start.1 = (bf16[128,2304]{1,0:T(8,128)(2,1)S(1)}, bf16[128,2304]{1,0:T(8,128)(2,1)S(1)}, u32[]{:S(2)}, u32[]{:S(2)}) collective-permute-start(bf16[128,2304]{1,0:T(8,128)(2,1)S(1)} %get-tuple-element.20), channel_id=1, source_target_pairs={{0,1},{1,2},{2,3},{3,4},{4,5},{5,6},{6,7},{7,8},{8,9},{9,10},{10,1... | collective-permute-start | bytes 1769480 | tf_op jit(solution)/shard_map/ppermute | solution.py:275
  44.7 11.2 %collective-permute-start.2 = (bf16[128,2304]{1,0:T(8,128)(2,1)S(1)}, bf16[128,2304]{1,0:T(8,128)(2,1)S(1)}, u32[]{:S(2)}, u32[]{:S(2)}) collective-permute-start(bf16[128,2304]{1,0:T(8,128)(2,1)S(1)} %get-tuple-element.21), channel_id=1, source_target_pairs={{1,0},{2,1},{3,2},{4,3},{5,4},{6,5},{7,6},{8,7},{9,8},{10,9},{11,1... | collective-permute-start | bytes 1769480 | tf_op jit(solution)/shard_map/ppermute | solution.py:276
  47.4 17.1 %all-to-all-start.2 = ((bf16[32,32,128]{2,1,0:T(8,128)(2,1)}), bf16[32,32,128]{2,1,0:T(8,128)(2,1)S(1)}, u32[]{:S(2)}, u32[]{:S(2)}) async-start(bf16[32,32,128]{2,1,0:T(8,128)(2,1)} %shard_map.57), calls=%async_computation.2 | async-start | bytes 524288 | tf_op jit(solution)/shard_map/all_to_all | solution.py:281
  54.9 0.8 %copy-start.2 = (bf16[128,2304]{1,0:T(8,128)(2,1)}, bf16[128,2304]{1,0:T(8,128)(2,1)S(1)}, u32[]{:S(2)}) copy-start(bf16[128,2304]{1,0:T(8,128)(2,1)S(1)} %collective-permute-done.1.before_ref) | copy-start | bytes 1769476
  55.9 0.8 %copy-start.4 = (bf16[128,2304]{1,0:T(8,128)(2,1)}, bf16[128,2304]{1,0:T(8,128)(2,1)S(1)}, u32[]{:S(2)}) copy-start(bf16[128,2304]{1,0:T(8,128)(2,1)S(1)} %collective-permute-done.2.after_ref) | copy-start | bytes 1769476
  56.8 1.3 %copy-start.1 = (bf16[16,2,8,2240]{3,2,1,0:T(8,128)(2,1)S(1)}, bf16[16,2,8,2240]{3,2,1,0:T(8,128)(2,1)}, u32[]{:S(2)}) copy-start(bf16[16,2,8,2240]{3,2,1,0:T(8,128)(2,1)} %param.5) | copy-start | bytes 3440644
  58.0 1.1 %copy-start.3 = (bf16[128,2304]{1,0:T(8,128)(2,1)S(1)}, bf16[128,2304]{1,0:T(8,128)(2,1)}, u32[]{:S(2)}) copy-start(bf16[128,2304]{1,0:T(8,128)(2,1)} %copy-done.2) | copy-start | bytes 1769476
  59.1 1.1 %copy-start.5 = (bf16[128,2304]{1,0:T(8,128)(2,1)S(1)}, bf16[128,2304]{1,0:T(8,128)(2,1)}, u32[]{:S(2)}) copy-start(bf16[128,2304]{1,0:T(8,128)(2,1)} %copy-done.4) | copy-start | bytes 1769476
  64.5 7.4 %collective-permute-start.3 = (bf16[1024,128]{1,0:T(8,128)(2,1)S(1)}, bf16[1024,128]{1,0:T(8,128)(2,1)S(1)}, u32[]{:S(2)}, u32[]{:S(2)}) collective-permute-start(bf16[1024,128]{1,0:T(8,128)(2,1)S(1)} %bitcast.8), channel_id=1, source_target_pairs={{0,1},{1,0},{2,3},{3,2},{4,5},{5,4},{6,7},{7,6},{8,9},{9,8},{10,11... | collective-permute-start | bytes 786440 | tf_op jit(solution)/shard_map/ppermute | solution.py:289

commit v4 on v3

--- a/solution.py
+++ b/solution.py
@@ -74,26 +74,30 @@
 
 
 def totals_kernel(pieces_ref, out_ref):
-    zs, xs = out_ref.shape[:2]
-    ys = pieces_ref.shape[0] // xs
+    zs = out_ref.shape[0]
+    pieces, chunk = pieces_ref.shape[:2]
+    xs = out_ref.shape[1] // chunk
+    ys = pieces // xs
     for x in range(xs):
         total = pieces_ref[ys * x].astype(F32)
         for y in range(1, ys):
             total = total + pieces_ref[ys * x + y].astype(F32)
         total = total.astype(BF16)
         for z in range(zs):
-            out_ref[z, x] = total
+            out_ref[z, chunk * x : chunk * (x + 1), :] = total
 
 
 def prefix_kernel(place_ref, blocks_ref, out_ref):
-    zs, xs = blocks_ref.shape[:2]
-    ys = out_ref.shape[0] // xs
+    zs = blocks_ref.shape[0]
+    pieces, chunk = out_ref.shape[:2]
+    xs = blocks_ref.shape[1] // chunk
+    ys = pieces // xs
     place = place_ref[0]
-    before = jnp.zeros(blocks_ref.shape[2:], F32)
+    before = jnp.zeros((chunk, LANES), F32)
     for x in range(xs):
         upto, whole = before, before
         for z in range(zs):
-            block = blocks_ref[z, x].astype(F32)
+            block = blocks_ref[z, chunk * x : chunk * (x + 1), :].astype(F32)
             upto = upto + jnp.where(z <= place, block, 0.0)
             whole = whole + block
         state = upto.astype(BF16)
@@ -130,12 +134,9 @@
 
 
 def readout_kernel(
-    core_ref, q_ref, mine_ref, other_ref, rows_ref, out_ref, state_ref, attn_ref, scale_ref, taps, out_buf, sems
+    q_ref, state_ref, rows_ref, out_ref, attn_ref, scale_ref, taps, out_buf, sems
 ):
-    core = core_ref[0]
     tokens = q_ref.shape[0] // 2
-    state_ref[core] = mine_ref[...]
-    state_ref[1 - core] = other_ref[...]
     lane = lax.broadcasted_iota(jnp.int32, (HEAD, LANES), 1)
     zero = jnp.zeros((HEAD, LANES), BF16)
 
@@ -243,7 +244,6 @@
     tokens = frames * rows * cols
     shape = jax.ShapeDtypeStruct
     core = lax.axis_index("core").reshape(1).astype(jnp.int32)
-    swap = [(0, 1), (1, 0)]
 
     mine, other = call(
         state_kernel,
@@ -262,9 +262,10 @@
 
     xs, ys, zs = lax.axis_size("x"), lax.axis_size("y"), lax.axis_size("z")
     chunk = HALF_ROWS // (xs * ys)
-    half = (mine + lax.ppermute(other, "core", swap).astype(F32)).astype(BF16)
+    both = lax.all_gather(other, "core")
+    half = (mine + jnp.where(core == 0, both[1], both[0]).astype(F32)).astype(BF16)
     pieces = lax.all_to_all(half.reshape(xs * ys, chunk, LANES), ("x", "y"), 0, 0, tiled=True)
-    totals = call(totals_kernel, shape((zs, xs, chunk, LANES), BF16), [VM], VM)(pieces)
+    totals = call(totals_kernel, shape((zs, xs * chunk, LANES), BF16), [VM], VM)(pieces)
 
     totals, q_late = lax.optimization_barrier((totals, queries.reshape(tokens, width)))
     border = shape((tokens // 2, TILES * LANES), BF16)
@@ -286,23 +287,22 @@
         [VM] * 2,
     )(q_late, q_before, q_after, gain.reshape(1, width), conv_weight)
     held, by_head, taps = lax.optimization_barrier((held.reshape(HALF_ROWS, LANES), by_head, taps))
-    taken = lax.ppermute(held, "core", swap)
+    state = lax.all_gather(held, "core")
 
     padded = TILES * LANES
     out = call(
         readout_kernel,
         shape((tokens, width), BF16),
-        [SM] + [VM] * 4,
+        [VM] * 3,
         HB,
         [
-            pltpu.VMEM((2, HALF_ROWS, LANES), BF16),
             pltpu.VMEM((2 * tokens, padded), F32),
             pltpu.VMEM((2 * tokens, LANES), F32),
             pltpu.VMEM((9, 8, padded), F32),
             pltpu.VMEM((tokens, width), BF16),
             pltpu.SemaphoreType.DMA((CHUNKS,)),
         ],
-    )(core, by_head, held, taken, taps)
+    )(by_head, state, taps)
     return out.reshape(frames, rows, cols, width)
 
 

time: 76.8 us -> 74.5 us (0.970)
  starting transfers between devices: 41.5 us -> 25.9 us
  blocking collectives: 13.8 us -> 28.8 us
  local copies, waits for them, and re-layouts: 5.06 us -> 3.17 us
  Pallas kernels: 10 us -> 10.8 us
    all_gather x0 -> x2, blocking collectives: none -> 15 us  [the longest x1 8.69 us: shards(): both = lax.all_gather(other, 'core')]
    ppermute x2 -> x0, starting transfers between devices: 15 us -> none  [the longest x1 8.79 us: shards(): half = (mine + lax.ppermute(other, 'core', swap).astype(F32)).astype(BF16)]
    ppermute x2 -> x0, waiting for transfers between devices: 2.28 us -> none  [the longest x1 1.14 us: shards(): half = (mine + lax.ppermute(other, 'core', swap).astype(F32)).astype(BF16)]
    unnamed x16 -> x12, local copies, waits for them, and re-layouts: 5.05 us -> 3.16 us
    ppermute x1, waiting for transfers between devices: 0.18 us -> 1.64 us  [shards(): q_after = lax.ppermute(top, ('y', 'core'), down)]
    pallas_call x1, Pallas kernels: 0.28 us -> 1.08 us  [shards(): call(border_kernel, [border] * 2, [VM], [VM] * 2, flops=20000000000)(q_late)]
  transfers between devices with their start and end apart: 6 -> 4, of which waited for: 4 -> 2; matrix products, arithmetic and copies ran while one was open for 0% -> 0% of each run, Pallas kernels for 3% -> 4%
where the time goes in v4:
time: 74.5 us; the launch traced here: 74.1 us
  blocking collectives  28.8 us (39%)
  starting transfers between devices  25.9 us (35%)
  Pallas kernels  10.8 us (14%)
  waiting for transfers between devices  5.24 us (7%)
  local copies, waits for them, and re-layouts  3.17 us (4%)
    all_to_all x1, blocking collectives, shards(): lax.all_to_all(half.reshape(xs * ys, chunk, LANES), ('x', 'y'), 0, 0, til...  13.8 us
    all_to_all x1, starting transfers between devices, shards(): blocks = lax.all_to_all(totals, 'z', 0, 0, tiled=True)  10 us
    all_gather x1, blocking collectives, shards(): both = lax.all_gather(other, 'core')  8.69 us
    ppermute x1, starting transfers between devices, shards(): q_before = lax.ppermute(low, ('y', 'core'), up)  7.14 us
    all_to_all x1, starting transfers between devices, shards(): held = lax.all_to_all(prefix, ('x', 'y'), 0, 0, tiled=True)  6.79 us
    all_gather x1, blocking collectives, shards(): state = lax.all_gather(held, 'core')  6.32 us
    pallas_call x1, Pallas kernels, shards(): call(readout_kernel, shape((tokens, width), BF16), [VM] * 3, HB, [pltpu.V...  4.3 us
    all_to_all x1, waiting for transfers between devices, shards(): held = lax.all_to_all(prefix, ('x', 'y'), 0, 0, tiled=True)  3.59 us
  transfers between devices with their start and end apart: 4, of which 2 were waited for; matrix products, arithmetic and copies ran while one was open for 0% of the time, Pallas kernels for 4%

profile of v4, /device:TPU:1, one launch (start us, length us, event | category | flops | bytes accessed | tf_op | source)
XLA Modules:
  0.0 74.1 jit_solution(537550394212064225)
XLA Ops:
  0.0 2.7 %shard_map.55 = (f32[1024,128]{1,0:T(8,128)S(1)}, bf16[1024,128]{1,0:T(8,128)(2,1)S(1)}) custom-call(s32[1]{0:T(128)} %bitcast.1.core_ref, bf16[256,2240]{1,0:T(8,128)(2,1)} %bitcast.14, bf16[256,2240]{1,0:T(8,128)(2,1)} %bitcast.15), custom_call_target="tpu_custom_call" | custom-call | flops 1000000000 | bytes 5000000 | tf_op jit(solution)/shard_map/pallas_call | solution.py:248
  2.7 8.7 %all-gather = bf16[2048,128]{1,0:T(8,128)(2,1)S(1)} all-gather(bf16[1024,128]{1,0:T(8,128)(2,1)S(1)} %get-tuple-element.17), channel_id=2, replica_groups=mesh['x'=4,'z'=8,'y'=8,'core'=2] {'core'}, dimensions={0}, use_global_device_ids=true | all-gather | bytes 786432 | tf_op jit(solution)/shard_map/all_gather | solution.py:265
  11.4 0.1 fusion
  11.5 13.8 %all_to_all.15.pieces_ref = bf16[32,32,128]{2,1,0:T(8,128)(2,1)S(1)} all-to-all(bf16[32,32,128]{2,1,0:T(8,128)(2,1)S(1)} %bitcast.13), channel_id=1, replica_groups=mesh['x'=4,'z'=8,'y'=8,'core'=2] {'x','y'}, dimensions={0} | all-to-all | bytes 524288 | tf_op jit(solution)/shard_map/all_to_all | solution.py:267
  25.3 0.0 copy-start
  25.3 0.7 %shard_map.56 = bf16[8,128,128]{2,1,0:T(8,128)(2,1)} custom-call(bf16[32,32,128]{2,1,0:T(8,128)(2,1)S(1)} %all_to_all.15.pieces_ref), custom_call_target="tpu_custom_call" | custom-call | flops 1000000000 | bytes 5000000 | tf_op jit(solution)/shard_map/pallas_call | solution.py:268
  26.0 10.0 %all-to-all-start.1 = ((bf16[8,128,128]{2,1,0:T(8,128)(2,1)}), bf16[8,128,128]{2,1,0:T(8,128)(2,1)S(1)}, u32[]{:S(2)}, u32[]{:S(2)}) async-start(bf16[8,128,128]{2,1,0:T(8,128)(2,1)} %shard_map.56), calls=%async_computation.1 | async-start | bytes 524288 | tf_op jit(solution)/shard_map/all_to_all | solution.py:279
  36.0 0.0 copy-done
  36.0 0.0 copy-start.5
  36.0 0.0 copy-start.4
  36.1 1.1 %shard_map.58 = (bf16[128,2304]{1,0:T(8,128)(2,1)S(1)}, bf16[128,2304]{1,0:T(8,128)(2,1)}) custom-call(bf16[256,2240]{1,0:T(8,128)(2,1)S(1)} %bitcast.11), custom_call_target="tpu_custom_call" | custom-call | flops 20000000000 | bytes 5000000 | tf_op jit(solution)/shard_map/pallas_call | solution.py:272
  37.1 7.1 %collective-permute-start = (bf16[128,2304]{1,0:T(8,128)(2,1)}, bf16[128,2304]{1,0:T(8,128)(2,1)S(1)}, u32[]{:S(2)}, u32[]{:S(2)}) collective-permute-start(bf16[128,2304]{1,0:T(8,128)(2,1)} %get-tuple-element.20), channel_id=1, source_target_pairs={{0,1},{1,2},{2,3},{3,4},{4,5},{5,6},{6,7},{7,8},{8,9},{9,10},{10,1... | collective-permute-start | bytes 1769480 | tf_op jit(solution)/shard_map/ppermute | solution.py:276
  44.3 1.9 %collective-permute-start.1 = (bf16[128,2304]{1,0:T(8,128)(2,1)S(1)}, bf16[128,2304]{1,0:T(8,128)(2,1)S(1)}, u32[]{:S(2)}, u32[]{:S(2)}) collective-permute-start(bf16[128,2304]{1,0:T(8,128)(2,1)S(1)} %get-tuple-element.21), channel_id=1, source_target_pairs={{1,0},{2,1},{3,2},{4,3},{5,4},{6,5},{7,6},{8,7},{9,8},{10,9},{11,1... | collective-permute-start | bytes 1769480 | tf_op jit(solution)/shard_map/ppermute | solution.py:277
  46.2 0.0 all-to-all-done.1.blocks_ref
  46.2 0.8 %shard_map.57 = bf16[32,32,128]{2,1,0:T(8,128)(2,1)} custom-call(s32[1]{0:T(128)} %bitcast.place_ref, bf16[8,128,128]{2,1,0:T(8,128)(2,1)S(1)} %all-to-all-done.1.blocks_ref), custom_call_target="tpu_custom_call" | custom-call | flops 100000000 | bytes 5000000 | tf_op jit(solution)/shard_map/pallas_call | solution.py:281
  47.0 6.8 %all-to-all-start.2 = ((bf16[32,32,128]{2,1,0:T(8,128)(2,1)}), bf16[32,32,128]{2,1,0:T(8,128)(2,1)}, u32[]{:S(2)}, u32[]{:S(2)}) async-start(bf16[32,32,128]{2,1,0:T(8,128)(2,1)} %shard_map.57), calls=%async_computation.2 | async-start | bytes 524288 | tf_op jit(solution)/shard_map/all_to_all | solution.py:282
  53.8 0.0 copy-done.5
  53.8 0.0 collective-permute-done.before_ref
  53.8 1.6 %collective-permute-done.1.after_ref = bf16[128,2304]{1,0:T(8,128)(2,1)S(1)} collective-permute-done((bf16[128,2304]{1,0:T(8,128)(2,1)S(1)}, bf16[128,2304]{1,0:T(8,128)(2,1)S(1)}, u32[]{:S(2)}, u32[]{:S(2)}) %collective-permute-start.1) | collective-permute-done | bytes 589856 | tf_op jit(solution)/shard_map/ppermute | solution.py:277
  55.5 0.0 copy-start.2
  55.5 0.8 %copy-done.2 = bf16[128,2304]{1,0:T(8,128)(2,1)} copy-done((bf16[128,2304]{1,0:T(8,128)(2,1)}, bf16[128,2304]{1,0:T(8,128)(2,1)S(1)}, u32[]{:S(2)}) %copy-start.2) | copy-done | bytes 589848
  56.3 0.0 copy-done.4
  56.3 0.0 copy-start.1
  56.3 1.3 %copy-done.1 = bf16[16,2,8,2240]{3,2,1,0:T(8,128)(2,1)S(1)} copy-done((bf16[16,2,8,2240]{3,2,1,0:T(8,128)(2,1)S(1)}, bf16[16,2,8,2240]{3,2,1,0:T(8,128)(2,1)}, u32[]{:S(2)}) %copy-start.1) | copy-done | bytes 1146904
  57.6 0.0 copy-start.3
  57.6 1.1 %copy-done.3 = bf16[128,2304]{1,0:T(8,128)(2,1)S(1)} copy-done((bf16[128,2304]{1,0:T(8,128)(2,1)S(1)}, bf16[128,2304]{1,0:T(8,128)(2,1)}, u32[]{:S(2)}) %copy-start.3) | copy-done | bytes 589848
  58.6 1.2 %shard_map.59 = (bf16[512,2560]{1,0:T(8,128)(2,1)S(1)}, f32[16,2304]{1,0:T(8,128)S(1)}) custom-call(bf16[256,2240]{1,0:T(8,128)(2,1)S(1)} %bitcast.12, bf16[128,2304]{1,0:T(8,128)(2,1)S(1)} %collective-permute-done.before_ref, bf16[128,2304]{1,0:T(8,128)(2,1)S(1)} %copy-done.3, f32[1,2240]{1,0:T(1,128)S(1)} %reshape.39.gain_ref, f32[9,2240]{1,0:T(8,128)S(1)} %copy-done.4), custom_call_target="tpu_custom_call" | custom-call | flops 1000000000 | bytes 5000000 | tf_op jit(solution)/shard_map/pallas_call | solution.py:283
  59.9 3.6 %all-to-all-done.2 = bf16[32,32,128]{2,1,0:T(8,128)(2,1)} async-done(((bf16[32,32,128]{2,1,0:T(8,128)(2,1)}), bf16[32,32,128]{2,1,0:T(8,128)(2,1)}, u32[]{:S(2)}, u32[]{:S(2)}) %all-to-all-start.2) | async-done | bytes 262176 | tf_op jit(solution)/shard_map/all_to_all | solution.py:282
  63.4 6.3 %all-gather.1 = bf16[2048,128]{1,0:T(8,128)(2,1)S(1)} all-gather(bf16[1024,128]{1,0:T(8,128)(2,1)} %bitcast.7), channel_id=3, replica_groups=mesh['x'=4,'z'=8,'y'=8,'core'=2] {'core'}, dimensions={0}, use_global_device_ids=true | all-gather | bytes 786432 | tf_op jit(solution)/shard_map/all_gather | solution.py:290
  69.8 4.3 %shard_map.60 = bf16[256,2240]{1,0:T(8,128)(2,1)} custom-call(bf16[512,2560]{1,0:T(8,128)(2,1)S(1)} %get-tuple-element.24.q_ref, bf16[2,1024,128]{2,1,0:T(8,128)(2,1)S(1)} %bitcast.10, f32[16,2304]{1,0:T(8,128)S(1)} %get-tuple-element.26.rows_ref), custom_call_target="tpu_custom_call" | custom-call | flops 1000000000 | bytes 5000000 | tf_op jit(solution)/shard_map/pallas_call | solution.py:293
  (1 shorter events, 0.0 us)
Async XLA Ops:
  25.3 10.8 %copy-start = (bf16[16,2,8,2240]{3,2,1,0:T(8,128)(2,1)S(1)}, bf16[16,2,8,2240]{3,2,1,0:T(8,128)(2,1)}, u32[]{:S(2)}) copy-start(bf16[16,2,8,2240]{3,2,1,0:T(8,128)(2,1)} %param.5) | copy-start | bytes 3440644
  26.0 20.2 %all-to-all-start.1 = ((bf16[8,128,128]{2,1,0:T(8,128)(2,1)}), bf16[8,128,128]{2,1,0:T(8,128)(2,1)S(1)}, u32[]{:S(2)}, u32[]{:S(2)}) async-start(bf16[8,128,128]{2,1,0:T(8,128)(2,1)} %shard_map.56), calls=%async_computation.1 | async-start | bytes 524288 | tf_op jit(solution)/shard_map/all_to_all | solution.py:279
  36.0 17.8 %copy-start.5 = (f32[2240]{0:T(1024)S(1)}, f32[2240]{0:T(1024)}, u32[]{:S(2)}) copy-start(f32[2240]{0:T(1024)} %param.8) | copy-start | bytes 26884
  36.0 20.3 %copy-start.4 = (f32[9,2240]{1,0:T(8,128)S(1)}, f32[9,2240]{1,0:T(8,128)}, u32[]{:S(2)}) copy-start(f32[9,2240]{1,0:T(8,128)} %weight_ref.1) | copy-start | bytes 241924
  37.1 16.7 %collective-permute-start = (bf16[128,2304]{1,0:T(8,128)(2,1)}, bf16[128,2304]{1,0:T(8,128)(2,1)S(1)}, u32[]{:S(2)}, u32[]{:S(2)}) collective-permute-start(bf16[128,2304]{1,0:T(8,128)(2,1)} %get-tuple-element.20), channel_id=1, source_target_pairs={{0,1},{1,2},{2,3},{3,4},{4,5},{5,6},{6,7},{7,8},{8,9},{9,10},{10,1... | collective-permute-start | bytes 1769480 | tf_op jit(solution)/shard_map/ppermute | solution.py:276
  44.3 11.2 %collective-permute-start.1 = (bf16[128,2304]{1,0:T(8,128)(2,1)S(1)}, bf16[128,2304]{1,0:T(8,128)(2,1)S(1)}, u32[]{:S(2)}, u32[]{:S(2)}) collective-permute-start(bf16[128,2304]{1,0:T(8,128)(2,1)S(1)} %get-tuple-element.21), channel_id=1, source_target_pairs={{1,0},{2,1},{3,2},{4,3},{5,4},{6,5},{7,6},{8,7},{9,8},{10,9},{11,1... | collective-permute-start | bytes 1769480 | tf_op jit(solution)/shard_map/ppermute | solution.py:277
  47.0 16.4 %all-to-all-start.2 = ((bf16[32,32,128]{2,1,0:T(8,128)(2,1)}), bf16[32,32,128]{2,1,0:T(8,128)(2,1)}, u32[]{:S(2)}, u32[]{:S(2)}) async-start(bf16[32,32,128]{2,1,0:T(8,128)(2,1)} %shard_map.57), calls=%async_computation.2 | async-start | bytes 524288 | tf_op jit(solution)/shard_map/all_to_all | solution.py:282
  55.5 0.8 %copy-start.2 = (bf16[128,2304]{1,0:T(8,128)(2,1)}, bf16[128,2304]{1,0:T(8,128)(2,1)S(1)}, u32[]{:S(2)}) copy-start(bf16[128,2304]{1,0:T(8,128)(2,1)S(1)} %collective-permute-done.1.after_ref) | copy-start | bytes 1769476
  56.3 1.3 %copy-start.1 = (bf16[16,2,8,2240]{3,2,1,0:T(8,128)(2,1)S(1)}, bf16[16,2,8,2240]{3,2,1,0:T(8,128)(2,1)}, u32[]{:S(2)}) copy-start(bf16[16,2,8,2240]{3,2,1,0:T(8,128)(2,1)} %param.5) | copy-start | bytes 3440644
  57.6 1.1 %copy-start.3 = (bf16[128,2304]{1,0:T(8,128)(2,1)S(1)}, bf16[128,2304]{1,0:T(8,128)(2,1)}, u32[]{:S(2)}) copy-start(bf16[128,2304]{1,0:T(8,128)(2,1)} %copy-done.2) | copy-start | bytes 1769476

commit v5 on v4

--- a/solution.py
+++ b/solution.py
@@ -45,10 +45,15 @@
     for tile in range(TILES):
         low, high = lane_range(tile)
         kt_ref[low:high, :] = jnp.maximum(k_buf[:, low:high], 0).T
+    lane = lax.broadcasted_iota(jnp.int32, (HEAD, LANES), 1)
+    ones = jnp.ones((tokens, LANES), BF16)
+    last_end = tile_heads(TILES - 1)[1]
+    sums = jnp.zeros((HEAD, LANES), F32)
+    for head in range(HEADS):
+        ksum = jnp.dot(kt_ref[HEAD * head : HEAD * (head + 1), :], ones, preferred_element_type=F32)
+        sums = jnp.where(lane == last_end + head, ksum, sums)
     for copy in copies[CHUNKS:]:
         copy.wait()
-    lane = lax.broadcasted_iota(jnp.int32, (HEAD, LANES), 1)
-    ones = jnp.ones((tokens, LANES), BF16)
     for tile in range(TILES):
         first, end = tile_heads(tile)
         low, high = lane_range(tile)
@@ -59,11 +64,7 @@
         else:
             v = jnp.concatenate([v, jnp.zeros((tokens, LANES - v.shape[1]), BF16)], axis=1)
             state = jnp.dot(kt_ref[HEAD * first : WIDTH, :], v, preferred_element_type=F32)
-            for head in range(HEADS):
-                ksum = jnp.dot(
-                    kt_ref[HEAD * head : HEAD * (head + 1), :], ones, preferred_element_type=F32
-                )
-                state = jnp.where(lane == end + head, ksum, state)
+            state = jnp.where(lane < end, state, sums)
         half, place = divmod(tile, HALF_TILES)
         state_ref[half, HEAD * place : HEAD * (place + 1), :] = state
     rest = HEAD * HALF_TILES
@@ -264,10 +265,7 @@
     chunk = HALF_ROWS // (xs * ys)
     both = lax.all_gather(other, "core")
     half = (mine + jnp.where(core == 0, both[1], both[0]).astype(F32)).astype(BF16)
-    pieces = lax.all_to_all(half.reshape(xs * ys, chunk, LANES), ("x", "y"), 0, 0, tiled=True)
-    totals = call(totals_kernel, shape((zs, xs * chunk, LANES), BF16), [VM], VM)(pieces)
-
-    totals, q_late = lax.optimization_barrier((totals, queries.reshape(tokens, width)))
+    half, q_late = lax.optimization_barrier((half, queries.reshape(tokens, width)))
     border = shape((tokens // 2, TILES * LANES), BF16)
     top, low = call(border_kernel, [border] * 2, [VM], [VM] * 2, flops=20_000_000_000)(q_late)
     size = ys * 2
@@ -276,17 +274,21 @@
     q_before = lax.ppermute(low, ("y", "core"), up)
     q_after = lax.ppermute(top, ("y", "core"), down)
 
+    pieces = lax.all_to_all(half.reshape(xs * ys, chunk, LANES), ("x", "y"), 0, 0, tiled=True)
+    totals = call(totals_kernel, shape((zs, xs * chunk, LANES), BF16), [VM], VM)(pieces)
+
     blocks = lax.all_to_all(totals, "z", 0, 0, tiled=True)
-    place = lax.axis_index("z").reshape(1).astype(jnp.int32)
-    prefix = call(prefix_kernel, shape((xs * ys, chunk, LANES), BF16), [SM, VM], VM, flops=PREFIX_FLOPS)(place, blocks)
-    held = lax.all_to_all(prefix, ("x", "y"), 0, 0, tiled=True)
     by_head, taps = call(
         heads_kernel,
         [shape((2 * tokens, HEADS * LANES), BF16), shape((16, TILES * LANES), F32)],
         [VM] * 5,
         [VM] * 2,
     )(q_late, q_before, q_after, gain.reshape(1, width), conv_weight)
-    held, by_head, taps = lax.optimization_barrier((held.reshape(HALF_ROWS, LANES), by_head, taps))
+    blocks, by_head, taps = lax.optimization_barrier((blocks, by_head, taps))
+    place = lax.axis_index("z").reshape(1).astype(jnp.int32)
+    prefix = call(prefix_kernel, shape((xs * ys, chunk, LANES), BF16), [SM, VM], VM, flops=PREFIX_FLOPS)(place, blocks)
+    held = lax.all_to_all(prefix, ("x", "y"), 0, 0, tiled=True)
+    held = held.reshape(HALF_ROWS, LANES)
     state = lax.all_gather(held, "core")
 
     padded = TILES * LANES

time: 74.5 us -> 74.2 us (level)
  starting transfers between devices: 25.9 us -> 20.3 us
  blocking collectives: 28.8 us -> 31.8 us
  local copies, waits for them, and re-layouts: 3.17 us -> 5.05 us
  Pallas kernels: 10.8 us -> 9.17 us
  waiting for transfers between devices: 5.24 us -> 6.42 us
    ppermute x1, starting transfers between devices: 7.14 us -> 3.96 us  [shards(): q_before = lax.ppermute(low, ('y', 'core'), up)]
    all_to_all x1, waiting for transfers between devices: 0.01 us -> 3.09 us  [shards(): blocks = lax.all_to_all(totals, 'z', 0, 0, tiled=True)]
    all_to_all x1, blocking collectives: 13.8 us -> 16.8 us  [shards(): held = lax.all_to_all(prefix, ('x', 'y'), 0, 0, tiled=True)]
    all_to_all x1, starting transfers between devices: 6.79 us -> 4.31 us  [shards(): lax.all_to_all(half.reshape(xs * ys, chunk, LANES), ('x', 'y'), 0, 0, til...]
    unnamed x12 -> x16, local copies, waits for them, and re-layouts: 3.16 us -> 5.04 us
    ppermute x1, waiting for transfers between devices: 1.64 us -> 0.01 us  [shards(): q_after = lax.ppermute(top, ('y', 'core'), down)]
    pallas_call x1, Pallas kernels: 1.08 us -> 0.28 us  [shards(): call(border_kernel, [border] * 2, [VM], [VM] * 2, flops=20000000000)(q_late)]
  transfers between devices with their start and end apart: 4 -> 4, of which waited for: 2 -> 2; matrix products, arithmetic and copies ran while one was open for 0% -> 0% of each run, Pallas kernels for 4% -> 3%
where the time goes in v5:
time: 74.2 us; the launch traced here: 73.7 us
  blocking collectives  31.8 us (43%)
  starting transfers between devices  20.3 us (27%)
  Pallas kernels  9.17 us (12%)
  waiting for transfers between devices  6.42 us (9%)
  local copies, waits for them, and re-layouts  5.05 us (7%)
  other arithmetic  0.79 us (1%)
    all_to_all x1, blocking collectives, shards(): held = lax.all_to_all(prefix, ('x', 'y'), 0, 0, tiled=True)  16.8 us
    all_to_all x1, starting transfers between devices, shards(): blocks = lax.all_to_all(totals, 'z', 0, 0, tiled=True)  10 us
    all_gather x1, blocking collectives, shards(): both = lax.all_gather(other, 'core')  8.82 us
    all_gather x1, blocking collectives, shards(): state = lax.all_gather(held, 'core')  6.14 us
    unnamed x16, local copies, waits for them, and re-layouts  5.04 us
    all_to_all x1, starting transfers between devices, shards(): lax.all_to_all(half.reshape(xs * ys, chunk, LANES), ('x', 'y'), 0, 0, til...  4.31 us
    pallas_call x1, Pallas kernels, shards(): call(readout_kernel, shape((tokens, width), BF16), [VM] * 3, HB, [pltpu.V...  4.3 us
    ppermute x1, starting transfers between devices, shards(): q_before = lax.ppermute(low, ('y', 'core'), up)  3.96 us
  transfers between devices with their start and end apart: 4, of which 2 were waited for; matrix products, arithmetic and copies ran while one was open for 0% of the time, Pallas kernels for 3%

profile of v5, /device:TPU:1, one launch (start us, length us, event | category | flops | bytes accessed | tf_op | source)
XLA Modules:
  0.0 73.7 jit_solution(4089957106633379451)
XLA Ops:
  0.0 2.6 %shard_map.55 = (f32[1024,128]{1,0:T(8,128)S(1)}, bf16[1024,128]{1,0:T(8,128)(2,1)S(1)}) custom-call(s32[1]{0:T(128)} %bitcast.core_ref, bf16[256,2240]{1,0:T(8,128)(2,1)} %bitcast.12, bf16[256,2240]{1,0:T(8,128)(2,1)} %bitcast.13), custom_call_target="tpu_custom_call" | custom-call | flops 1000000000 | bytes 5000000 | tf_op jit(solution)/shard_map/pallas_call | solution.py:249
  2.6 0.0 copy-start
  2.6 8.8 %all-gather = bf16[2048,128]{1,0:T(8,128)(2,1)S(1)} all-gather(bf16[1024,128]{1,0:T(8,128)(2,1)S(1)} %get-tuple-element.17), channel_id=2, replica_groups=mesh['x'=4,'z'=8,'y'=8,'core'=2] {'core'}, dimensions={0}, use_global_device_ids=true | all-gather | bytes 786432 | tf_op jit(solution)/shard_map/all_gather | solution.py:266
  11.4 0.8 %fusion = bf16[1024,128]{1,0:T(8,128)(2,1)} fusion(f32[1024,128]{1,0:T(8,128)S(1)} %get-tuple-element.16, bf16[2048,128]{1,0:T(8,128)(2,1)S(1)} %all-gather, pred[]{:T(512)} %bitcast.3), kind=kLoop, calls=%fused_computation.1 | loop fusion | flops 524288 | bytes 1310721 | tf_op jit(solution)/shard_map/convert_element_type | solution.py:267
  12.2 4.3 %all-to-all-start = ((bf16[32,32,128]{2,1,0:T(8,128)(2,1)}), bf16[32,32,128]{2,1,0:T(8,128)(2,1)S(1)}, u32[]{:S(2)}, u32[]{:S(2)}) async-start(bf16[32,32,128]{2,1,0:T(8,128)(2,1)} %bitcast.5), calls=%async_computation | async-start | bytes 524288 | tf_op jit(solution)/shard_map/all_to_all | solution.py:277
  16.5 0.0 copy-done
  16.5 0.3 shard_map.57
  16.8 4.0 %collective-permute-start = (bf16[128,2304]{1,0:T(8,128)(2,1)S(1)}, bf16[128,2304]{1,0:T(8,128)(2,1)S(1)}, u32[]{:S(2)}, u32[]{:S(2)}) collective-permute-start(bf16[128,2304]{1,0:T(8,128)(2,1)S(1)} %get-tuple-element.20), channel_id=1, source_target_pairs={{0,1},{1,2},{2,3},{3,4},{4,5},{5,6},{6,7},{7,8},{8,9},{9,10},{10,1... | collective-permute-start | bytes 1769480 | tf_op jit(solution)/shard_map/ppermute | solution.py:274
  20.8 0.0 copy-start.7
  20.8 0.0 copy-start.6
  20.8 2.1 %collective-permute-start.1 = (bf16[128,2304]{1,0:T(8,128)(2,1)S(1)}, bf16[128,2304]{1,0:T(8,128)(2,1)S(1)}, u32[]{:S(2)}, u32[]{:S(2)}) collective-permute-start(bf16[128,2304]{1,0:T(8,128)(2,1)S(1)} %get-tuple-element.21), channel_id=1, source_target_pairs={{1,0},{2,1},{3,2},{4,3},{5,4},{6,5},{7,6},{8,7},{9,8},{10,9},{11,1... | collective-permute-start | bytes 1769480 | tf_op jit(solution)/shard_map/ppermute | solution.py:275
  22.9 3.3 %all-to-all-done.pieces_ref = bf16[32,32,128]{2,1,0:T(8,128)(2,1)S(1)} async-done(((bf16[32,32,128]{2,1,0:T(8,128)(2,1)}), bf16[32,32,128]{2,1,0:T(8,128)(2,1)S(1)}, u32[]{:S(2)}, u32[]{:S(2)}) %all-to-all-start) | async-done | bytes 262176 | tf_op jit(solution)/shard_map/all_to_all | solution.py:277
  26.2 0.7 %shard_map.56 = bf16[8,128,128]{2,1,0:T(8,128)(2,1)} custom-call(bf16[32,32,128]{2,1,0:T(8,128)(2,1)S(1)} %all-to-all-done.pieces_ref), custom_call_target="tpu_custom_call" | custom-call | flops 1000000000 | bytes 5000000 | tf_op jit(solution)/shard_map/pallas_call | solution.py:278
  26.9 10.0 %all-to-all-start.1 = ((bf16[8,128,128]{2,1,0:T(8,128)(2,1)}), bf16[8,128,128]{2,1,0:T(8,128)(2,1)S(1)}, u32[]{:S(2)}, u32[]{:S(2)}) async-start(bf16[8,128,128]{2,1,0:T(8,128)(2,1)} %shard_map.56), calls=%async_computation.1 | async-start | bytes 524288 | tf_op jit(solution)/shard_map/all_to_all | solution.py:280
  37.0 0.0 copy-done.7
  37.0 0.0 collective-permute-done.before_ref
  37.0 0.0 copy-start.2
  37.0 0.8 %copy-done.2 = bf16[128,2304]{1,0:T(8,128)(2,1)} copy-done((bf16[128,2304]{1,0:T(8,128)(2,1)}, bf16[128,2304]{1,0:T(8,128)(2,1)S(1)}, u32[]{:S(2)}) %copy-start.2) | copy-done | bytes 589848
  37.8 0.0 collective-permute-done.1.after_ref
  37.8 0.0 copy-start.4
  37.8 0.8 %copy-done.4 = bf16[128,2304]{1,0:T(8,128)(2,1)} copy-done((bf16[128,2304]{1,0:T(8,128)(2,1)}, bf16[128,2304]{1,0:T(8,128)(2,1)S(1)}, u32[]{:S(2)}) %copy-start.4) | copy-done | bytes 589848
  38.6 0.0 copy-done.6
  38.6 0.0 copy-start.1
  38.6 1.3 %copy-done.1 = bf16[16,2,8,2240]{3,2,1,0:T(8,128)(2,1)S(1)} copy-done((bf16[16,2,8,2240]{3,2,1,0:T(8,128)(2,1)S(1)}, bf16[16,2,8,2240]{3,2,1,0:T(8,128)(2,1)}, u32[]{:S(2)}) %copy-start.1) | copy-done | bytes 1146904
  39.9 0.0 copy-start.3
  39.9 1.1 %copy-done.3 = bf16[128,2304]{1,0:T(8,128)(2,1)S(1)} copy-done((bf16[128,2304]{1,0:T(8,128)(2,1)S(1)}, bf16[128,2304]{1,0:T(8,128)(2,1)}, u32[]{:S(2)}) %copy-start.3) | copy-done | bytes 589848
  41.0 0.0 copy-start.5
  41.0 1.1 %copy-done.5 = bf16[128,2304]{1,0:T(8,128)(2,1)S(1)} copy-done((bf16[128,2304]{1,0:T(8,128)(2,1)S(1)}, bf16[128,2304]{1,0:T(8,128)(2,1)}, u32[]{:S(2)}) %copy-start.5) | copy-done | bytes 589848
  42.0 1.2 %shard_map.58 = (bf16[512,2560]{1,0:T(8,128)(2,1)S(1)}, f32[16,2304]{1,0:T(8,128)S(1)}) custom-call(bf16[256,2240]{1,0:T(8,128)(2,1)S(1)} %bitcast.10, bf16[128,2304]{1,0:T(8,128)(2,1)S(1)} %copy-done.3, bf16[128,2304]{1,0:T(8,128)(2,1)S(1)} %copy-done.5, f32[1,2240]{1,0:T(1,128)S(1)} %reshape.34.gain_ref, f32[9,2240]{1,0:T(8,128)S(1)} %copy-done.6), custom_call_target="tpu_custom_call" | custom-call | flops 1000000000 | bytes 5000000 | tf_op jit(solution)/shard_map/pallas_call | solution.py:281
  43.3 3.1 %all-to-all-done.1.blocks_ref = bf16[8,128,128]{2,1,0:T(8,128)(2,1)S(1)} async-done(((bf16[8,128,128]{2,1,0:T(8,128)(2,1)}), bf16[8,128,128]{2,1,0:T(8,128)(2,1)S(1)}, u32[]{:S(2)}, u32[]{:S(2)}) %all-to-all-start.1) | async-done | bytes 262176 | tf_op jit(solution)/shard_map/all_to_all | solution.py:280
  46.3 0.1 shard_map.59
  46.4 16.8 %all_to_all.15 = bf16[32,32,128]{2,1,0:T(8,128)(2,1)S(1)} all-to-all(bf16[32,32,128]{2,1,0:T(8,128)(2,1)S(1)} %shard_map.59), channel_id=1, replica_groups=mesh['x'=4,'z'=8,'y'=8,'core'=2] {'x','y'}, dimensions={0} | all-to-all | bytes 524288 | tf_op jit(solution)/shard_map/all_to_all | solution.py:290
  63.2 6.1 %all_gather.11.state_ref = bf16[2,1024,128]{2,1,0:T(8,128)(2,1)S(1)} all-gather(bf16[1,1024,128]{2,1,0:T(8,128)(2,1)S(1)} %bitcast.11), channel_id=1, replica_groups=mesh['x'=4,'z'=8,'y'=8,'core'=2] {'core'}, dimensions={0}, use_global_device_ids=true | all-gather | bytes 786432 | tf_op jit(solution)/shard_map/all_gather | solution.py:292
  69.4 4.3 %shard_map.60 = bf16[256,2240]{1,0:T(8,128)(2,1)} custom-call(bf16[512,2560]{1,0:T(8,128)(2,1)S(1)} %get-tuple-element.24.q_ref, bf16[2,1024,128]{2,1,0:T(8,128)(2,1)S(1)} %all_gather.11.state_ref, f32[16,2304]{1,0:T(8,128)S(1)} %get-tuple-element.26.rows_ref), custom_call_target="tpu_custom_call" | custom-call | flops 1000000000 | bytes 5000000 | tf_op jit(solution)/shard_map/pallas_call | solution.py:295
  (1 shorter events, 0.0 us)
Async XLA Ops:
  2.6 13.9 %copy-start = (bf16[16,2,8,2240]{3,2,1,0:T(8,128)(2,1)S(1)}, bf16[16,2,8,2240]{3,2,1,0:T(8,128)(2,1)}, u32[]{:S(2)}) copy-start(bf16[16,2,8,2240]{3,2,1,0:T(8,128)(2,1)} %param.5) | copy-start | bytes 3440644
  12.2 14.0 %all-to-all-start = ((bf16[32,32,128]{2,1,0:T(8,128)(2,1)}), bf16[32,32,128]{2,1,0:T(8,128)(2,1)S(1)}, u32[]{:S(2)}, u32[]{:S(2)}) async-start(bf16[32,32,128]{2,1,0:T(8,128)(2,1)} %bitcast.5), calls=%async_computation | async-start | bytes 524288 | tf_op jit(solution)/shard_map/all_to_all | solution.py:277
  16.8 20.2 %collective-permute-start = (bf16[128,2304]{1,0:T(8,128)(2,1)S(1)}, bf16[128,2304]{1,0:T(8,128)(2,1)S(1)}, u32[]{:S(2)}, u32[]{:S(2)}) collective-permute-start(bf16[128,2304]{1,0:T(8,128)(2,1)S(1)} %get-tuple-element.20), channel_id=1, source_target_pairs={{0,1},{1,2},{2,3},{3,4},{4,5},{5,6},{6,7},{7,8},{8,9},{9,10},{10,1... | collective-permute-start | bytes 1769480 | tf_op jit(solution)/shard_map/ppermute | solution.py:274
  20.8 16.2 %copy-start.7 = (f32[2240]{0:T(1024)S(1)}, f32[2240]{0:T(1024)}, u32[]{:S(2)}) copy-start(f32[2240]{0:T(1024)} %param.8) | copy-start | bytes 26884
  20.8 17.8 %copy-start.6 = (f32[9,2240]{1,0:T(8,128)S(1)}, f32[9,2240]{1,0:T(8,128)}, u32[]{:S(2)}) copy-start(f32[9,2240]{1,0:T(8,128)} %weight_ref.1) | copy-start | bytes 241924
  20.8 17.0 %collective-permute-start.1 = (bf16[128,2304]{1,0:T(8,128)(2,1)S(1)}, bf16[128,2304]{1,0:T(8,128)(2,1)S(1)}, u32[]{:S(2)}, u32[]{:S(2)}) collective-permute-start(bf16[128,2304]{1,0:T(8,128)(2,1)S(1)} %get-tuple-element.21), channel_id=1, source_target_pairs={{1,0},{2,1},{3,2},{4,3},{5,4},{6,5},{7,6},{8,7},{9,8},{10,9},{11,1... | collective-permute-start | bytes 1769480 | tf_op jit(solution)/shard_map/ppermute | solution.py:275
  26.9 19.4 %all-to-all-start.1 = ((bf16[8,128,128]{2,1,0:T(8,128)(2,1)}), bf16[8,128,128]{2,1,0:T(8,128)(2,1)S(1)}, u32[]{:S(2)}, u32[]{:S(2)}) async-start(bf16[8,128,128]{2,1,0:T(8,128)(2,1)} %shard_map.56), calls=%async_computation.1 | async-start | bytes 524288 | tf_op jit(solution)/shard_map/all_to_all | solution.py:280
  37.0 0.8 %copy-start.2 = (bf16[128,2304]{1,0:T(8,128)(2,1)}, bf16[128,2304]{1,0:T(8,128)(2,1)S(1)}, u32[]{:S(2)}) copy-start(bf16[128,2304]{1,0:T(8,128)(2,1)S(1)} %collective-permute-done.before_ref) | copy-start | bytes 1769476
  37.8 0.8 %copy-start.4 = (bf16[128,2304]{1,0:T(8,128)(2,1)}, bf16[128,2304]{1,0:T(8,128)(2,1)S(1)}, u32[]{:S(2)}) copy-start(bf16[128,2304]{1,0:T(8,128)(2,1)S(1)} %collective-permute-done.1.after_ref) | copy-start | bytes 1769476
  38.6 1.3 %copy-start.1 = (bf16[16,2,8,2240]{3,2,1,0:T(8,128)(2,1)S(1)}, bf16[16,2,8,2240]{3,2,1,0:T(8,128)(2,1)}, u32[]{:S(2)}) copy-start(bf16[16,2,8,2240]{3,2,1,0:T(8,128)(2,1)} %param.5) | copy-start | bytes 3440644
  39.9 1.1 %copy-start.3 = (bf16[128,2304]{1,0:T(8,128)(2,1)S(1)}, bf16[128,2304]{1,0:T(8,128)(2,1)}, u32[]{:S(2)}) copy-start(bf16[128,2304]{1,0:T(8,128)(2,1)} %copy-done.2) | copy-start | bytes 1769476
  41.0 1.1 %copy-start.5 = (bf16[128,2304]{1,0:T(8,128)(2,1)S(1)}, bf16[128,2304]{1,0:T(8,128)(2,1)}, u32[]{:S(2)}) copy-start(bf16[128,2304]{1,0:T(8,128)(2,1)} %copy-done.4) | copy-start | bytes 1769476

commit v6 on v5

--- a/solution.py
+++ b/solution.py
@@ -13,6 +13,7 @@
 HALF_TILES = TILES // 2
 PREFIX_FLOPS = 100_000_000
 STATE_VMEM = 55_200_000
+LOADS = 2
 CHUNKS = 4
 HALF_ROWS = 1024
 EPS = 1e-06
@@ -32,15 +33,15 @@
 def state_kernel(core_ref, k_ref, v_ref, mine_ref, other_ref, k_buf, v_buf, kt_ref, state_ref, sems):
     core = core_ref[0]
     tokens = k_buf.shape[0]
-    rows = tokens // CHUNKS
+    rows = tokens // LOADS
     copies = []
     for which, (ref, buf) in enumerate(((k_ref, k_buf), (v_ref, v_buf))):
-        for chunk in range(CHUNKS):
+        for chunk in range(LOADS):
             part = slice(rows * chunk, rows * (chunk + 1))
             copies.append(pltpu.make_async_copy(ref.at[part], buf.at[part], sems.at[which, chunk]))
     for copy in copies:
         copy.start()
-    for copy in copies[:CHUNKS]:
+    for copy in copies[:LOADS]:
         copy.wait()
     for tile in range(TILES):
         low, high = lane_range(tile)
@@ -52,7 +53,7 @@
     for head in range(HEADS):
         ksum = jnp.dot(kt_ref[HEAD * head : HEAD * (head + 1), :], ones, preferred_element_type=F32)
         sums = jnp.where(lane == last_end + head, ksum, sums)
-    for copy in copies[CHUNKS:]:
+    for copy in copies[LOADS:]:
         copy.wait()
     for tile in range(TILES):
         first, end = tile_heads(tile)
@@ -165,9 +166,6 @@
         q = q_ref[:, LANES * first : LANES * (first + len(heads))]
         both = jnp.dot(q, weights, preferred_element_type=F32)
         attn = both[:, :LANES] / (both[:, LANES:] + EPS)
-        if tile == TILES - 1:
-            keep = lax.broadcasted_iota(jnp.int32, attn.shape, 1) < end
-            attn = jnp.where(keep, attn, 0.0)
         square = square + attn * attn
         low, high = lane_range(tile)
         attn_ref[:, low:high] = attn[:, : high - low] * rows_ref[9:10, low:high]
@@ -256,7 +254,7 @@
             pltpu.VMEM((tokens, width), BF16),
             pltpu.VMEM((width, tokens), BF16),
             pltpu.VMEM((2, HEAD * HALF_TILES, LANES), F32),
-            pltpu.SemaphoreType.DMA((2, CHUNKS)),
+            pltpu.SemaphoreType.DMA((2, LOADS)),
         ],
         vmem=STATE_VMEM,
     )(core, keys.reshape(tokens, width), values.reshape(tokens, width))

time: 74.2 us -> 74.2 us (level)
  no operation moved by 1% of the time
where the time goes in v6:
time: 74.2 us; the launch traced here: 73.7 us
  blocking collectives  31.8 us (43%)
  starting transfers between devices  20.3 us (27%)
  Pallas kernels  9.15 us (12%)
  waiting for transfers between devices  6.42 us (9%)
  local copies, waits for them, and re-layouts  5.05 us (7%)
  other arithmetic  0.79 us (1%)
    all_to_all x1, blocking collectives, shards(): held = lax.all_to_all(prefix, ('x', 'y'), 0, 0, tiled=True)  16.8 us
    all_to_all x1, starting transfers between devices, shards(): blocks = lax.all_to_all(totals, 'z', 0, 0, tiled=True)  10 us
    all_gather x1, blocking collectives, shards(): both = lax.all_gather(other, 'core')  8.83 us
    all_gather x1, blocking collectives, shards(): state = lax.all_gather(held, 'core')  6.14 us
    unnamed x16, local copies, waits for them, and re-layouts  5.04 us
    pallas_call x1, Pallas kernels, shards(): call(readout_kernel, shape((tokens, width), BF16), [VM] * 3, HB, [pltpu.V...  4.3 us
    all_to_all x1, starting transfers between devices, shards(): lax.all_to_all(half.reshape(xs * ys, chunk, LANES), ('x', 'y'), 0, 0, til...  4.29 us
    ppermute x1, starting transfers between devices, shards(): q_before = lax.ppermute(low, ('y', 'core'), up)  3.96 us
  transfers between devices with their start and end apart: 4, of which 2 were waited for; matrix products, arithmetic and copies ran while one was open for 0% of the time, Pallas kernels for 3%

profile of v6, /device:TPU:1, one launch (start us, length us, event | category | flops | bytes accessed | tf_op | source)
XLA Modules:
  0.0 73.7 jit_solution(14671743027545932458)
XLA Ops:
  0.0 2.6 %shard_map.55 = (f32[1024,128]{1,0:T(8,128)S(1)}, bf16[1024,128]{1,0:T(8,128)(2,1)S(1)}) custom-call(s32[1]{0:T(128)} %bitcast.core_ref, bf16[256,2240]{1,0:T(8,128)(2,1)} %bitcast.12, bf16[256,2240]{1,0:T(8,128)(2,1)} %bitcast.13), custom_call_target="tpu_custom_call" | custom-call | flops 1000000000 | bytes 5000000 | tf_op jit(solution)/shard_map/pallas_call | solution.py:247
  2.6 0.0 copy-start
  2.6 8.8 %all-gather = bf16[2048,128]{1,0:T(8,128)(2,1)S(1)} all-gather(bf16[1024,128]{1,0:T(8,128)(2,1)S(1)} %get-tuple-element.17), channel_id=2, replica_groups=mesh['x'=4,'z'=8,'y'=8,'core'=2] {'core'}, dimensions={0}, use_global_device_ids=true | all-gather | bytes 786432 | tf_op jit(solution)/shard_map/all_gather | solution.py:264
  11.4 0.8 %fusion = bf16[1024,128]{1,0:T(8,128)(2,1)} fusion(f32[1024,128]{1,0:T(8,128)S(1)} %get-tuple-element.16, bf16[2048,128]{1,0:T(8,128)(2,1)S(1)} %all-gather, pred[]{:T(512)} %bitcast.3), kind=kLoop, calls=%fused_computation.1 | loop fusion | flops 524288 | bytes 1310721 | tf_op jit(solution)/shard_map/convert_element_type | solution.py:265
  12.2 4.3 %all-to-all-start = ((bf16[32,32,128]{2,1,0:T(8,128)(2,1)}), bf16[32,32,128]{2,1,0:T(8,128)(2,1)S(1)}, u32[]{:S(2)}, u32[]{:S(2)}) async-start(bf16[32,32,128]{2,1,0:T(8,128)(2,1)} %bitcast.5), calls=%async_computation | async-start | bytes 524288 | tf_op jit(solution)/shard_map/all_to_all | solution.py:275
  16.5 0.0 copy-done
  16.5 0.3 shard_map.57
  16.8 4.0 %collective-permute-start = (bf16[128,2304]{1,0:T(8,128)(2,1)S(1)}, bf16[128,2304]{1,0:T(8,128)(2,1)S(1)}, u32[]{:S(2)}, u32[]{:S(2)}) collective-permute-start(bf16[128,2304]{1,0:T(8,128)(2,1)S(1)} %get-tuple-element.20), channel_id=1, source_target_pairs={{0,1},{1,2},{2,3},{3,4},{4,5},{5,6},{6,7},{7,8},{8,9},{9,10},{10,1... | collective-permute-start | bytes 1769480 | tf_op jit(solution)/shard_map/ppermute | solution.py:272
  20.8 0.0 copy-start.7
  20.8 0.0 copy-start.6
  20.8 2.1 %collective-permute-start.1 = (bf16[128,2304]{1,0:T(8,128)(2,1)S(1)}, bf16[128,2304]{1,0:T(8,128)(2,1)S(1)}, u32[]{:S(2)}, u32[]{:S(2)}) collective-permute-start(bf16[128,2304]{1,0:T(8,128)(2,1)S(1)} %get-tuple-element.21), channel_id=1, source_target_pairs={{1,0},{2,1},{3,2},{4,3},{5,4},{6,5},{7,6},{8,7},{9,8},{10,9},{11,1... | collective-permute-start | bytes 1769480 | tf_op jit(solution)/shard_map/ppermute | solution.py:273
  22.8 3.3 %all-to-all-done.pieces_ref = bf16[32,32,128]{2,1,0:T(8,128)(2,1)S(1)} async-done(((bf16[32,32,128]{2,1,0:T(8,128)(2,1)}), bf16[32,32,128]{2,1,0:T(8,128)(2,1)S(1)}, u32[]{:S(2)}, u32[]{:S(2)}) %all-to-all-start) | async-done | bytes 262176 | tf_op jit(solution)/shard_map/all_to_all | solution.py:275
  26.2 0.7 %shard_map.56 = bf16[8,128,128]{2,1,0:T(8,128)(2,1)} custom-call(bf16[32,32,128]{2,1,0:T(8,128)(2,1)S(1)} %all-to-all-done.pieces_ref), custom_call_target="tpu_custom_call" | custom-call | flops 1000000000 | bytes 5000000 | tf_op jit(solution)/shard_map/pallas_call | solution.py:276
  26.9 10.0 %all-to-all-start.1 = ((bf16[8,128,128]{2,1,0:T(8,128)(2,1)}), bf16[8,128,128]{2,1,0:T(8,128)(2,1)S(1)}, u32[]{:S(2)}, u32[]{:S(2)}) async-start(bf16[8,128,128]{2,1,0:T(8,128)(2,1)} %shard_map.56), calls=%async_computation.1 | async-start | bytes 524288 | tf_op jit(solution)/shard_map/all_to_all | solution.py:278
  37.0 0.0 copy-done.7
  37.0 0.0 collective-permute-done.before_ref
  37.0 0.0 copy-start.2
  37.0 0.8 %copy-done.2 = bf16[128,2304]{1,0:T(8,128)(2,1)} copy-done((bf16[128,2304]{1,0:T(8,128)(2,1)}, bf16[128,2304]{1,0:T(8,128)(2,1)S(1)}, u32[]{:S(2)}) %copy-start.2) | copy-done | bytes 589848
  37.8 0.0 collective-permute-done.1.after_ref
  37.8 0.0 copy-start.4
  37.8 0.8 %copy-done.4 = bf16[128,2304]{1,0:T(8,128)(2,1)} copy-done((bf16[128,2304]{1,0:T(8,128)(2,1)}, bf16[128,2304]{1,0:T(8,128)(2,1)S(1)}, u32[]{:S(2)}) %copy-start.4) | copy-done | bytes 589848
  38.6 0.0 copy-done.6
  38.6 0.0 copy-start.1
  38.6 1.3 %copy-done.1 = bf16[16,2,8,2240]{3,2,1,0:T(8,128)(2,1)S(1)} copy-done((bf16[16,2,8,2240]{3,2,1,0:T(8,128)(2,1)S(1)}, bf16[16,2,8,2240]{3,2,1,0:T(8,128)(2,1)}, u32[]{:S(2)}) %copy-start.1) | copy-done | bytes 1146904
  39.9 0.0 copy-start.3
  39.9 1.1 %copy-done.3 = bf16[128,2304]{1,0:T(8,128)(2,1)S(1)} copy-done((bf16[128,2304]{1,0:T(8,128)(2,1)S(1)}, bf16[128,2304]{1,0:T(8,128)(2,1)}, u32[]{:S(2)}) %copy-start.3) | copy-done | bytes 589848
  41.0 0.0 copy-start.5
  41.0 1.1 %copy-done.5 = bf16[128,2304]{1,0:T(8,128)(2,1)S(1)} copy-done((bf16[128,2304]{1,0:T(8,128)(2,1)S(1)}, bf16[128,2304]{1,0:T(8,128)(2,1)}, u32[]{:S(2)}) %copy-start.5) | copy-done | bytes 589848
  42.0 1.2 %shard_map.58 = (bf16[512,2560]{1,0:T(8,128)(2,1)S(1)}, f32[16,2304]{1,0:T(8,128)S(1)}) custom-call(bf16[256,2240]{1,0:T(8,128)(2,1)S(1)} %bitcast.10, bf16[128,2304]{1,0:T(8,128)(2,1)S(1)} %copy-done.3, bf16[128,2304]{1,0:T(8,128)(2,1)S(1)} %copy-done.5, f32[1,2240]{1,0:T(1,128)S(1)} %reshape.34.gain_ref, f32[9,2240]{1,0:T(8,128)S(1)} %copy-done.6), custom_call_target="tpu_custom_call" | custom-call | flops 1000000000 | bytes 5000000 | tf_op jit(solution)/shard_map/pallas_call | solution.py:279
  43.2 3.1 %all-to-all-done.1.blocks_ref = bf16[8,128,128]{2,1,0:T(8,128)(2,1)S(1)} async-done(((bf16[8,128,128]{2,1,0:T(8,128)(2,1)}), bf16[8,128,128]{2,1,0:T(8,128)(2,1)S(1)}, u32[]{:S(2)}, u32[]{:S(2)}) %all-to-all-start.1) | async-done | bytes 262176 | tf_op jit(solution)/shard_map/all_to_all | solution.py:278
  46.3 0.1 shard_map.59
  46.4 16.8 %all_to_all.15 = bf16[32,32,128]{2,1,0:T(8,128)(2,1)S(1)} all-to-all(bf16[32,32,128]{2,1,0:T(8,128)(2,1)S(1)} %shard_map.59), channel_id=1, replica_groups=mesh['x'=4,'z'=8,'y'=8,'core'=2] {'x','y'}, dimensions={0} | all-to-all | bytes 524288 | tf_op jit(solution)/shard_map/all_to_all | solution.py:288
  63.2 6.1 %all_gather.11.state_ref = bf16[2,1024,128]{2,1,0:T(8,128)(2,1)S(1)} all-gather(bf16[1,1024,128]{2,1,0:T(8,128)(2,1)S(1)} %bitcast.11), channel_id=1, replica_groups=mesh['x'=4,'z'=8,'y'=8,'core'=2] {'core'}, dimensions={0}, use_global_device_ids=true | all-gather | bytes 786432 | tf_op jit(solution)/shard_map/all_gather | solution.py:290
  69.4 4.3 %shard_map.60 = bf16[256,2240]{1,0:T(8,128)(2,1)} custom-call(bf16[512,2560]{1,0:T(8,128)(2,1)S(1)} %get-tuple-element.24.q_ref, bf16[2,1024,128]{2,1,0:T(8,128)(2,1)S(1)} %all_gather.11.state_ref, f32[16,2304]{1,0:T(8,128)S(1)} %get-tuple-element.26.rows_ref), custom_call_target="tpu_custom_call" | custom-call | flops 1000000000 | bytes 5000000 | tf_op jit(solution)/shard_map/pallas_call | solution.py:293
  (1 shorter events, 0.0 us)
Async XLA Ops:
  2.6 13.9 %copy-start = (bf16[16,2,8,2240]{3,2,1,0:T(8,128)(2,1)S(1)}, bf16[16,2,8,2240]{3,2,1,0:T(8,128)(2,1)}, u32[]{:S(2)}) copy-start(bf16[16,2,8,2240]{3,2,1,0:T(8,128)(2,1)} %param.5) | copy-start | bytes 3440644
  12.2 14.0 %all-to-all-start = ((bf16[32,32,128]{2,1,0:T(8,128)(2,1)}), bf16[32,32,128]{2,1,0:T(8,128)(2,1)S(1)}, u32[]{:S(2)}, u32[]{:S(2)}) async-start(bf16[32,32,128]{2,1,0:T(8,128)(2,1)} %bitcast.5), calls=%async_computation | async-start | bytes 524288 | tf_op jit(solution)/shard_map/all_to_all | solution.py:275
  16.8 20.2 %collective-permute-start = (bf16[128,2304]{1,0:T(8,128)(2,1)S(1)}, bf16[128,2304]{1,0:T(8,128)(2,1)S(1)}, u32[]{:S(2)}, u32[]{:S(2)}) collective-permute-start(bf16[128,2304]{1,0:T(8,128)(2,1)S(1)} %get-tuple-element.20), channel_id=1, source_target_pairs={{0,1},{1,2},{2,3},{3,4},{4,5},{5,6},{6,7},{7,8},{8,9},{9,10},{10,1... | collective-permute-start | bytes 1769480 | tf_op jit(solution)/shard_map/ppermute | solution.py:272
  20.8 16.2 %copy-start.7 = (f32[2240]{0:T(1024)S(1)}, f32[2240]{0:T(1024)}, u32[]{:S(2)}) copy-start(f32[2240]{0:T(1024)} %param.8) | copy-start | bytes 26884
  20.8 17.9 %copy-start.6 = (f32[9,2240]{1,0:T(8,128)S(1)}, f32[9,2240]{1,0:T(8,128)}, u32[]{:S(2)}) copy-start(f32[9,2240]{1,0:T(8,128)} %weight_ref.1) | copy-start | bytes 241924
  20.8 17.0 %collective-permute-start.1 = (bf16[128,2304]{1,0:T(8,128)(2,1)S(1)}, bf16[128,2304]{1,0:T(8,128)(2,1)S(1)}, u32[]{:S(2)}, u32[]{:S(2)}) collective-permute-start(bf16[128,2304]{1,0:T(8,128)(2,1)S(1)} %get-tuple-element.21), channel_id=1, source_target_pairs={{1,0},{2,1},{3,2},{4,3},{5,4},{6,5},{7,6},{8,7},{9,8},{10,9},{11,1... | collective-permute-start | bytes 1769480 | tf_op jit(solution)/shard_map/ppermute | solution.py:273
  26.9 19.4 %all-to-all-start.1 = ((bf16[8,128,128]{2,1,0:T(8,128)(2,1)}), bf16[8,128,128]{2,1,0:T(8,128)(2,1)S(1)}, u32[]{:S(2)}, u32[]{:S(2)}) async-start(bf16[8,128,128]{2,1,0:T(8,128)(2,1)} %shard_map.56), calls=%async_computation.1 | async-start | bytes 524288 | tf_op jit(solution)/shard_map/all_to_all | solution.py:278
  37.0 0.8 %copy-start.2 = (bf16[128,2304]{1,0:T(8,128)(2,1)}, bf16[128,2304]{1,0:T(8,128)(2,1)S(1)}, u32[]{:S(2)}) copy-start(bf16[128,2304]{1,0:T(8,128)(2,1)S(1)} %collective-permute-done.before_ref) | copy-start | bytes 1769476
  37.8 0.8 %copy-start.4 = (bf16[128,2304]{1,0:T(8,128)(2,1)}, bf16[128,2304]{1,0:T(8,128)(2,1)S(1)}, u32[]{:S(2)}) copy-start(bf16[128,2304]{1,0:T(8,128)(2,1)S(1)} %collective-permute-done.1.after_ref) | copy-start | bytes 1769476
  38.6 1.3 %copy-start.1 = (bf16[16,2,8,2240]{3,2,1,0:T(8,128)(2,1)S(1)}, bf16[16,2,8,2240]{3,2,1,0:T(8,128)(2,1)}, u32[]{:S(2)}) copy-start(bf16[16,2,8,2240]{3,2,1,0:T(8,128)(2,1)} %param.5) | copy-start | bytes 3440644
  39.9 1.1 %copy-start.3 = (bf16[128,2304]{1,0:T(8,128)(2,1)S(1)}, bf16[128,2304]{1,0:T(8,128)(2,1)}, u32[]{:S(2)}) copy-start(bf16[128,2304]{1,0:T(8,128)(2,1)} %copy-done.2) | copy-start | bytes 1769476
  41.0 1.1 %copy-start.5 = (bf16[128,2304]{1,0:T(8,128)(2,1)S(1)}, bf16[128,2304]{1,0:T(8,128)(2,1)}, u32[]{:S(2)}) copy-start(bf16[128,2304]{1,0:T(8,128)(2,1)} %copy-done.4) | copy-start | bytes 1769476
